TPU v7x, 768 devices: a whole 4x8x12 slice. The times are simulated.
768 devices in a mesh: node: 48 (over z_lo, y), local: 16 (over x, z_hi, core).
Axes of the slice: x: 4, y: 8, z: 12 (z_hi: 2, z_lo: 6; z = z_hi * 6 + z_lo), core: 2. Of those that a mesh axis runs over, the one named last changes fastest.
Arguments:
- inputs: bfloat16 [98304, 8192], P(('node', 'local')), may hold values from -6 to 6
- key_grad: bfloat16 [98304, 1024], P(('node', 'local')), may hold values from -6 to 6
- weight_codes: bfloat16 [8192, 1024], P('local'), may hold values from -0.1875 to 0.1875
- weight_scales: float32 [64, 1024], P('local'), may hold values from 0.5 to 2
Outputs:
- input_grad: bfloat16 [98304, 8192], P(('node', 'local'))
- weight_grad: float32 [8192, 1024], P('local')
All inputs are finite; a program needn't handle non-finite values.
Results may differ from a plain program's by a relative error of at most 0.0049.
Values may be sent and summed in bfloat16 or wider, within the bound.
No kernel may reach another device: no remote copies, remote signals or barrier semaphores. Data moves between devices by JAX's collectives and lax.ppermute only.
A program may use at most 64 MiB of HBM per device.

v0:
```python
import math

import jax
import jax.numpy as jnp
from jax import lax
from jax.sharding import PartitionSpec as P

QBLOCK = 128


def local(inputs, key_grad, weight_codes, weight_scales):
    row_count, col_count = weight_codes.shape
    scale_rows = weight_scales.shape[0]
    weight = (
        (
            weight_codes.astype(jnp.float32).reshape(scale_rows, QBLOCK, col_count)
            * weight_scales[:, None, :]
        )
        .reshape(row_count, col_count)
        .astype(jnp.bfloat16)
    )
    total_tokens = key_grad.shape[0] * lax.axis_size("node") * lax.axis_size("local")
    factor = 1.0 / math.sqrt(total_tokens)
    everyone = lax.all_gather(key_grad, "local", axis=0, tiled=True)
    local_part = lax.dot_general(
        everyone, weight, (((1,), (1,)), ((), ())), preferred_element_type=jnp.float32
    ).astype(jnp.bfloat16)
    columns = lax.all_to_all(inputs, "local", split_axis=1, concat_axis=0, tiled=True)
    partial_value = (
        lax.dot_general(
            columns, everyone, (((0,), (0,)), ((), ())), preferred_element_type=jnp.float32
        )
        * factor
    )
    weight_grad = lax.psum(partial_value, "node")
    input_grad = lax.all_to_all(local_part, "local", split_axis=0, concat_axis=1, tiled=True)
    return (input_grad, weight_grad)


def solution(mesh):
    return jax.shard_map(
        local,
        mesh=mesh,
        in_specs=(
            P(("node", "local"), None),
            P(("node", "local"), None),
            P("local", None),
            P("local", None),
        ),
        out_specs=(P(("node", "local"), None), P("local", None)),
        check_vma=False,
    )
```

profile of v0, /device:TPU:8, one launch (start us, length us, event | category | flops | bytes accessed | tf_op | source)
XLA Modules:
  0.0 802.1 jit_solution(18098645883690320675)
XLA Ops:
  7.2 0.0 all-gather.2.cloned.1.call-start
  7.2 0.7 all-gather.2.cloned.1.call-update
  7.9 4.1 copy.12
  12.0 0.0 copy-start
  12.0 0.0 copy-start.1
  12.0 17.2 %all-to-all-start.1 = ((bf16[128,16,512]{0,2,1:T(8,128)(2,1)}), bf16[128,16,512]{0,2,1:T(8,128)(2,1)S(1)}, u32[]{:S(2)}, u32[]{:S(2)}) async-start(bf16[128,16,512]{0,2,1:T(8,128)(2,1)} %bitcast.21), calls=%async_computation.1 | async-start | bytes 4194304 | tf_op jit(solution)/shard_map/all_to_all | solution.py:28
  29.2 0.0 copy-done
  29.2 0.0 copy-done.1
  29.2 1.2 fusion
  30.4 138.9 %all-gather.2.cloned.1.call-done = bf16[2048,1024]{1,0:T(8,128)(2,1)} async-done(((bf16[128,1024]{1,0:T(8,128)(2,1)}), bf16[2048,1024]{1,0:T(8,128)(2,1)}) %all-gather.2.cloned.1.call-update) | async-done | bytes 4194320 | tf_op jit(solution)/shard_map/all_gather | solution.py:24
  169.3 4.9 fusion.1
  174.2 1.9 copy.17
  176.1 0.0 all-to-all-done.1
  176.1 4.4 all-to-all-start
  180.5 0.0 all-reduce.2.cloned.1.call-start
  180.6 2.6 copy.13
  183.2 6.5 convolution_multiply_fusion
  189.7 0.0 all-reduce.2.cloned.1.call-update
  189.7 62.8 %all-to-all-done = bf16[16,128,512]{1,2,0:T(8,128)(2,1)} async-done(((bf16[16,128,512]{1,2,0:T(8,128)(2,1)}), bf16[16,128,512]{1,2,0:T(8,128)(2,1)}, u32[]{:S(2)}, u32[]{:S(2)}) %all-to-all-start) | async-done | bytes 2097184 | tf_op jit(solution)/shard_map/all_to_all | solution.py:36
  252.5 4.1 copy.14
  256.6 535.5 %all-reduce.2.cloned.1.call-done = f32[512,1024]{1,0:T(8,128)} async-done(((f32[512,1024]{1,0:T(8,128)}), f32[512,1024]{1,0:T(8,128)}) %all-reduce.2.cloned.1.call-update) | async-done | bytes 2097168 | tf_op jit(solution)/shard_map/psum | solution.py:35
  792.1 3.2 copy.19
Async XLA Ops:
  7.2 162.2 %all-gather.2.cloned.1.call-start = ((), (), s32[]{:S(2)}) async-start(), calls=%async_computation.2 | async-start | bytes 4456448 | tf_op jit(solution)/shard_map/all_gather | solution.py:24
  12.0 17.2 %copy-start = (bf16[512,1024]{1,0:T(8,128)(2,1)S(1)}, bf16[512,1024]{1,0:T(8,128)(2,1)}, u32[]{:S(2)}) copy-start(bf16[512,1024]{1,0:T(8,128)(2,1)} %param.6) | copy-start | bytes 3145732
  12.0 17.2 %copy-start.1 = (f32[4,1024]{1,0:T(4,128)S(1)}, f32[4,1024]{1,0:T(4,128)}, u32[]{:S(2)}) copy-start(f32[4,1024]{1,0:T(4,128)} %param.7) | copy-start | bytes 49156
  12.0 164.1 %all-to-all-start.1 = ((bf16[128,16,512]{0,2,1:T(8,128)(2,1)}), bf16[128,16,512]{0,2,1:T(8,128)(2,1)S(1)}, u32[]{:S(2)}, u32[]{:S(2)}) async-start(bf16[128,16,512]{0,2,1:T(8,128)(2,1)} %bitcast.21), calls=%async_computation.1 | async-start | bytes 4194304 | tf_op jit(solution)/shard_map/all_to_all | solution.py:28
  176.1 76.4 %all-to-all-start = ((bf16[16,128,512]{1,2,0:T(8,128)(2,1)}), bf16[16,128,512]{1,2,0:T(8,128)(2,1)}, u32[]{:S(2)}, u32[]{:S(2)}) async-start(bf16[16,128,512]{1,2,0:T(8,128)(2,1)} %bitcast.19), calls=%async_computation | async-start | bytes 4194304 | tf_op jit(solution)/shard_map/all_to_all | solution.py:36
  180.5 611.5 %all-reduce.2.cloned.1.call-start = ((), (), s32[]{:S(2)}) async-start(), calls=%async_computation.3 | async-start | bytes 4194304 | tf_op jit(solution)/shard_map/psum | solution.py:35
Sparse Core Ops, SparseCore 0:
  11.8 157.4 all-gather.1
  189.8 602.1 all-reduce.1
where the time goes:
time: 802 us
  waiting for transfers between devices  738 us (92%)
  starting transfers between devices  21.7 us (3%)
  local copies, waits for them, and re-layouts  15.8 us (2%)
  between operations  14.1 us (2%)
  matrix products  11.4 us (1%)
    psum x1, waiting for transfers between devices, local(): weight_grad = lax.psum(partial_value, 'node')  535 us
    all_gather x1, waiting for transfers between devices, local(): everyone = lax.all_gather(key_grad, 'local', axis=0, tiled=True)  139 us
    all_to_all x1, waiting for transfers between devices, local(): lax.all_to_all(local_part, 'local', split_axis=0, concat_axis=1, tiled=True)  62.8 us
    all_to_all x1, starting transfers between devices, local(): lax.all_to_all(inputs, 'local', split_axis=1, concat_axis=0, tiled=True)  17.2 us
  transfers between devices with their start and end apart: 4, of which 3 were waited for; matrix products, arithmetic and copies ran while one was open for 3% of the time, Pallas kernels for 0%

commit v1 on v0

v1 whole, which is shorter than its diff:
```python
import math

import jax
import jax.numpy as jnp
from jax import lax
from jax.sharding import Mesh
from jax.sharding import PartitionSpec as P

QBLOCK = 128
AXES = ("zt", "zp", "y", "x", "zh", "c")
SIZES = (3, 2, 8, 4, 2, 2)
BF16 = jnp.bfloat16
F32 = jnp.float32


def swapped(value, axis):
    return lax.ppermute(value, axis, [(0, 1), (1, 0)])


def pair_in_order(mine, other, position, axis):
    first = jnp.where(position == 0, mine, other)
    second = jnp.where(position == 0, other, mine)
    return jnp.concatenate([first, second], axis=axis)


def local(inputs, key_grad, weight_codes, weight_scales):
    tokens, width = inputs.shape
    rows, cols = weight_codes.shape
    scale_rows = weight_scales.shape[0]
    zp, y, x, zh, c = (lax.axis_index(a) for a in ("zp", "y", "x", "zh", "c"))
    nx, ny, nt = 4, 8, 3
    half = rows // 2
    piece = half // ny
    total_tokens = tokens * math.prod(SIZES)
    factor = 1.0 / math.sqrt(total_tokens)

    with jax.named_scope("weight"):
        weight = (
            (
                weight_codes.astype(F32).reshape(scale_rows, QBLOCK, cols)
                * weight_scales[:, None, :]
            )
            .reshape(rows, cols)
            .astype(BF16)
        )
        share = rows // ny
        mine = lax.dynamic_slice_in_dim(weight, y * share, share, 0)
        theirs = swapped(mine, "zh")
        weight_other = lax.all_gather(theirs, "y", axis=0, tiled=True)
        weights = pair_in_order(weight, weight_other, zh, 0)

    with jax.named_scope("key_grads"):
        both = pair_in_order(key_grad[None], swapped(key_grad, "zp")[None], zp, 0)
        others = [
            lax.ppermute(both, "x", [(i, i ^ k) for i in range(nx)]) for k in (1, 3, 2)
        ]
        by_distance = [both, others[0], others[2], others[1]]
        slots = []
        for i in range(nx):
            value = by_distance[0]
            for k in range(1, nx):
                value = jnp.where((x ^ i) == k, by_distance[k], value)
            slots.append(value)
        column = jnp.stack(slots, axis=1)
        keys = pair_in_order(column[None], swapped(column, "c")[None], c, 0)

    with jax.named_scope("inputs"):
        sent = inputs.reshape(tokens, nx, 2, 2, 2, half)
        sent = sent.transpose(3, 4, 1, 0, 2, 5).reshape(4 * nx, tokens, 2 * half)
        got = lax.all_to_all(sent, ("c", "zp", "x"), 0, 0, tiled=True)

    with jax.named_scope("input_grad"):
        own = lax.dynamic_index_in_dim(keys, zp, 1, keepdims=False)
        local_part = lax.dot_general(
            own.reshape(2 * nx * tokens, cols),
            weights,
            (((1,), (1,)), ((), ())),
            preferred_element_type=F32,
        ).astype(BF16)
        back = lax.all_to_all(
            local_part.reshape(2 * nx, tokens, 2 * rows), ("c", "x"), 0, 0, tiled=True
        )
        input_grad = (
            back.reshape(2, nx, tokens, 2, rows).transpose(2, 1, 3, 0, 4).reshape(tokens, width)
        )

    with jax.named_scope("weight_grad"):
        partial_value = lax.dot_general(
            got.reshape(4 * nx * tokens, 2 * half),
            keys.reshape(4 * nx * tokens, cols),
            (((0,), (0,)), ((), ())),
            preferred_element_type=F32,
        ) * factor
        chunks = (
            partial_value.reshape(2, ny, piece, cols).transpose(1, 0, 2, 3).astype(BF16)
        )
        total = lax.dynamic_index_in_dim(chunks, y, 0, keepdims=False).astype(F32)
        for k in (4, 3, 5, 2, 6, 1, 7):
            out = lax.dynamic_index_in_dim(chunks, lax.rem(y + k, ny), 0, keepdims=False)
            came = lax.ppermute(out, "y", [(i, (i + k) % ny) for i in range(ny)])
            total = total + came.astype(F32)
        spread = jnp.broadcast_to(total.astype(BF16)[None], (nt, 2, piece, cols))
        spread = lax.all_to_all(
            spread.reshape(nt * 2, piece, cols), ("zt", "zh"), 0, 0, tiled=True
        )
        summed = spread.astype(F32).sum(axis=0).astype(BF16)
        spread = jnp.broadcast_to(summed[None], (2 * ny, piece, cols))
        gathered = lax.all_to_all(spread, ("zp", "y"), 0, 0, tiled=True)
        weight_grad = gathered.reshape(rows, cols).astype(F32)
    return (input_grad, weight_grad)


def solution(mesh):
    fine = Mesh(mesh.devices.reshape(SIZES), AXES)
    tokens_over = P(AXES, None)
    rows_over = P(("x", "zh", "c"), None)
    return jax.shard_map(
        local,
        mesh=fine,
        in_specs=(tokens_over, tokens_over, rows_over, rows_over),
        out_specs=(tokens_over, rows_over),
        check_vma=False,
    )
```

time: 802 us -> 273 us (0.34)
  waiting for transfers between devices: 738 us -> 120 us
  starting transfers between devices: 21.7 us -> 90.1 us
  local copies, waits for them, and re-layouts: 15.8 us -> 26.5 us
  other arithmetic: 1.23 us -> 11.6 us
    psum x1 -> x0, waiting for transfers between devices: 535 us -> none  [local(): weight_grad = lax.psum(partial_value, 'node')]
    all_gather x1, waiting for transfers between devices: 139 us -> 0.01 us  [local(): weight_other = lax.all_gather(theirs, 'y', axis=0, tiled=True)]
    ppermute x0 -> x13, waiting for transfers between devices: none -> 65.8 us  [the longest x3 32.2 us: swapped(): return lax.ppermute(value, axis, [(0, 1), (1, 0)])]
    ppermute x0 -> x13, starting transfers between devices: none -> 58.6 us  [the longest x7 28.3 us: local(): came = lax.ppermute(out, 'y', [(i, (i + k) % ny) for i in range(ny)])]
    reshape x0 -> x3, local copies, waits for them, and re-layouts: none -> 10.4 us  [local(): back.reshape(2, nx, tokens, 2, rows).transpose(2, 1, 3, 0, 4)]
    all_to_all x2 -> x4, starting transfers between devices: 21.6 us -> 31.5 us  [the longest x1 10.7 us: local(): lax.all_to_all(spread.reshape(nt * 2, piece, cols), ('zt', 'zh'), 0, 0, t...]
    all_to_all x2 -> x4, waiting for transfers between devices: 62.8 us -> 54.2 us  [the longest x1 26.5 us: local(): lax.all_to_all(local_part.reshape(2 * nx, tokens, 2 * rows), ('c', 'x'),...]
  transfers between devices with their start and end apart: 4 -> 18, of which waited for: 3 -> 10; matrix products, arithmetic and copies ran while one was open for 3% -> 13% of each run, Pallas kernels for 0% -> 0%
where the time goes in v1:
time: 273 us; the launch traced here: 272 us
  waiting for transfers between devices  120 us (44%)
  starting transfers between devices  90.1 us (33%)
  local copies, waits for them, and re-layouts  26.5 us (10%)
  between operations  14.5 us (5%)
  other arithmetic  11.6 us (4%)
  matrix products  8.92 us (3%)
    ppermute x3, waiting for transfers between devices, swapped(): return lax.ppermute(value, axis, [(0, 1), (1, 0)])  32.2 us
    ppermute x7, starting transfers between devices, local(): came = lax.ppermute(out, 'y', [(i, (i + k) % ny) for i in range(ny)])  28.3 us
    all_to_all x1, waiting for transfers between devices, local(): lax.all_to_all(local_part.reshape(2 * nx, tokens, 2 * rows), ('c', 'x'),...  26.5 us
    ppermute x3, starting transfers between devices, swapped(): return lax.ppermute(value, axis, [(0, 1), (1, 0)])  20.5 us
    ppermute x3, waiting for transfers between devices, local(): lax.ppermute(both, 'x', [(i, i ^ k) for i in range(nx)])  20.5 us
    all_to_all x1, waiting for transfers between devices, local(): gathered = lax.all_to_all(spread, ('zp', 'y'), 0, 0, tiled=True)  16.9 us
    ppermute x7, waiting for transfers between devices, local(): came = lax.ppermute(out, 'y', [(i, (i + k) % ny) for i in range(ny)])  13.1 us
    all_to_all x1, waiting for transfers between devices, local(): lax.all_to_all(spread.reshape(nt * 2, piece, cols), ('zt', 'zh'), 0, 0, t...  10.8 us
  transfers between devices with their start and end apart: 18, of which 10 were waited for; matrix products, arithmetic and copies ran while one was open for 13% of the time, Pallas kernels for 0%

profile of v1, /device:TPU:8, one launch (start us, length us, event | category | flops | bytes accessed | tf_op | source)
XLA Modules:
  0.0 271.6 jit_solution(2234000597441025489)
XLA Ops:
  7.2 3.2 %copy.22 = bf16[128,8192]{0,1:T(8,128)(2,1)S(1)} copy(bf16[128,8192]{1,0:T(8,128)(2,1)} %param.4) | data formatting | bytes 4194304 | tf_op args[0]
  10.4 1.5 copy.23
  11.9 6.4 %all-to-all-start.1 = ((bf16[16,128,512]{1,2,0:T(8,128)(2,1)}), bf16[16,128,512]{1,2,0:T(8,128)(2,1)}, u32[]{:S(2)}, u32[]{:S(2)}) async-start(bf16[16,128,512]{1,2,0:T(8,128)(2,1)} %bitcast.18), calls=%async_computation.1 | async-start | bytes 4194304 | tf_op jit(solution)/shard_map/inputs/all_to_all | solution.py:70
  18.3 3.8 %collective-permute-start = (bf16[128,1024]{1,0:T(8,128)(2,1)S(1)}, bf16[128,1024]{1,0:T(8,128)(2,1)S(1)}, u32[]{:S(2)}, u32[]{:S(2)}) collective-permute-start(bf16[128,1024]{1,0:T(8,128)(2,1)S(1)} %copy-done.7), channel_id=1, source_target_pairs={{0,128},{128,0},{1,129},{129,1},{2,130},{130,2},{3,131},{131,3},{4... | collective-permute-start | bytes 786440 | tf_op jit(solution)/shard_map/key_grads/ppermute | solution.py:17
  22.1 27.9 %collective-permute-done = bf16[128,1024]{1,0:T(8,128)(2,1)S(1)} collective-permute-done((bf16[128,1024]{1,0:T(8,128)(2,1)S(1)}, bf16[128,1024]{1,0:T(8,128)(2,1)S(1)}, u32[]{:S(2)}, u32[]{:S(2)}) %collective-permute-start) | collective-permute-done | bytes 262176 | tf_op jit(solution)/shard_map/key_grads/ppermute | solution.py:17
  50.2 4.1 %collective-permute-start.1 = (bf16[2,128,1024]{2,1,0:T(8,128)(2,1)S(1)}, bf16[2,128,1024]{2,1,0:T(8,128)(2,1)S(1)}, u32[]{:S(2)}, u32[]{:S(2)}) collective-permute-start(bf16[2,128,1024]{2,1,0:T(8,128)(2,1)S(1)} %pad_maximum_fusion.2), channel_id=1, source_target_pairs={{0,12},{4,8},{8,4},{12,0},{1,13},{5,9},{9,5},{13,1},{2,14},{6,10},... | collective-permute-start | bytes 1572872 | tf_op jit(solution)/shard_map/key_grads/ppermute | solution.py:55
  54.3 3.6 %collective-permute-start.2 = (bf16[2,128,1024]{2,1,0:T(8,128)(2,1)S(1)}, bf16[2,128,1024]{2,1,0:T(8,128)(2,1)S(1)}, u32[]{:S(2)}, u32[]{:S(2)}) collective-permute-start(bf16[2,128,1024]{2,1,0:T(8,128)(2,1)S(1)} %pad_maximum_fusion.2), channel_id=1, source_target_pairs={{0,8},{4,12},{8,0},{12,4},{1,9},{5,13},{9,1},{13,5},{2,10},{6,14},... | collective-permute-start | bytes 1572872 | tf_op jit(solution)/shard_map/key_grads/ppermute | solution.py:55
  57.9 2.1 collective-permute-start.3
  60.0 17.9 %collective-permute-done.1 = bf16[2,128,1024]{2,1,0:T(8,128)(2,1)S(1)} collective-permute-done((bf16[2,128,1024]{2,1,0:T(8,128)(2,1)S(1)}, bf16[2,128,1024]{2,1,0:T(8,128)(2,1)S(1)}, u32[]{:S(2)}, u32[]{:S(2)}) %collective-permute-start.1) | collective-permute-done | bytes 524320 | tf_op jit(solution)/shard_map/key_grads/ppermute | solution.py:55
  78.0 2.5 collective-permute-done.3
  82.0 1.9 collective-permute-start.4
  83.9 1.5 fusion.5
  85.4 14.8 %collective-permute-start.5 = (bf16[64,1024]{1,0:T(8,128)(2,1)S(1)}, bf16[64,1024]{1,0:T(8,128)(2,1)S(1)}, u32[]{:S(2)}, u32[]{:S(2)}) collective-permute-start(bf16[64,1024]{1,0:T(8,128)(2,1)S(1)} %constant_dynamic-slice_fusion), channel_id=1, source_target_pairs={{0,2},{2,0},{1,3},{3,1},{4,6},{6,4},{5,7},{7,5},{8,10},{10,8},{9,1... | collective-permute-start | bytes 393224 | tf_op jit(solution)/shard_map/weight/ppermute | solution.py:17
  100.3 4.3 %collective-permute-done.5 = bf16[64,1024]{1,0:T(8,128)(2,1)S(1)} collective-permute-done((bf16[64,1024]{1,0:T(8,128)(2,1)S(1)}, bf16[64,1024]{1,0:T(8,128)(2,1)S(1)}, u32[]{:S(2)}, u32[]{:S(2)}) %collective-permute-start.5) | collective-permute-done | bytes 131104 | tf_op jit(solution)/shard_map/weight/ppermute | solution.py:17
  104.6 0.7 copy-done.9
  105.3 2.4 select_bitcast_fusion
  107.7 1.3 copy-done
  109.0 2.3 pad_maximum_fusion
  111.3 3.9 %copy.24 = bf16[16,128,512]{2,1,0:T(8,128)(2,1)} copy(bf16[16,128,512]{1,2,0:T(8,128)(2,1)} %all-to-all-done.1) | data formatting | bytes 4194304 | tf_op jit(solution)/shard_map/inputs/all_to_all | solution.py:70
  115.2 5.2 %multiply_convert_fusion = bf16[1024,512]{0,1:T(8,128)(2,1)S(1)} fusion(bf16[2048,1024]{1,0:T(8,128)(2,1)} %bitcast.66, bf16[2048,512]{1,0:T(8,128)(2,1)} %bitcast.69), kind=kOutput, calls=%fused_computation.12 | convolution fusion | flops 2148532224 | bytes 7340032 | tf_op jit(solution)/shard_map/weight_grad/dot_general | solution.py:88
  120.5 1.0 copy-done.6
  121.4 0.8 dynamic-slice_bitcast_fusion.6
  122.2 4.5 %collective-permute-start.12 = (bf16[2,32,1024]{2,1,0:T(8,128)(2,1)S(1)}, bf16[2,32,1024]{2,1,0:T(8,128)(2,1)S(1)}, u32[]{:S(2)}, u32[]{:S(2)}) collective-permute-start(bf16[2,32,1024]{2,1,0:T(8,128)(2,1)S(1)} %get-tuple-element.10), channel_id=1, source_target_pairs={{0,112},{16,0},{32,16},{48,32},{64,48},{80,64},{96,80},{112,96},{1... | collective-permute-start | bytes 393224 | tf_op jit(solution)/shard_map/weight_grad/ppermute | solution.py:100
  126.7 1.9 collective-permute-start.11
  128.6 5.9 %collective-permute-start.10 = (bf16[2,32,1024]{2,1,0:T(8,128)(2,1)}, bf16[2,32,1024]{2,1,0:T(8,128)(2,1)}, u32[]{:S(2)}, u32[]{:S(2)}) collective-permute-start(bf16[2,32,1024]{2,1,0:T(8,128)(2,1)} %get-tuple-element.12), channel_id=1, source_target_pairs={{0,96},{16,112},{32,0},{48,16},{64,32},{80,48},{96,64},{112,80},{1... | collective-permute-start | bytes 393224 | tf_op jit(solution)/shard_map/weight_grad/ppermute | solution.py:100
  134.5 1.9 collective-permute-start.9
  136.4 5.6 %collective-permute-start.8 = (bf16[2,32,1024]{2,1,0:T(8,128)(2,1)}, bf16[2,32,1024]{2,1,0:T(8,128)(2,1)}, u32[]{:S(2)}, u32[]{:S(2)}) collective-permute-start(bf16[2,32,1024]{2,1,0:T(8,128)(2,1)} %get-tuple-element.14), channel_id=1, source_target_pairs={{0,80},{16,96},{32,112},{48,0},{64,16},{80,32},{96,48},{112,64},{1... | collective-permute-start | bytes 393224 | tf_op jit(solution)/shard_map/weight_grad/ppermute | solution.py:100
  142.1 3.2 %collective-permute-start.7 = (bf16[2,32,1024]{2,1,0:T(8,128)(2,1)S(1)}, bf16[2,32,1024]{2,1,0:T(8,128)(2,1)}, u32[]{:S(2)}, u32[]{:S(2)}) collective-permute-start(bf16[2,32,1024]{2,1,0:T(8,128)(2,1)S(1)} %get-tuple-element.15), channel_id=1, source_target_pairs={{0,48},{16,64},{32,80},{48,96},{64,112},{80,0},{96,16},{112,32},{1... | collective-permute-start | bytes 393224 | tf_op jit(solution)/shard_map/weight_grad/ppermute | solution.py:100
  145.3 0.6 copy-done.8
  146.0 5.2 %collective-permute-start.6 = (bf16[2,32,1024]{2,1,0:T(8,128)(2,1)S(1)}, bf16[2,32,1024]{2,1,0:T(8,128)(2,1)}, u32[]{:S(2)}, u32[]{:S(2)}) collective-permute-start(bf16[2,32,1024]{2,1,0:T(8,128)(2,1)S(1)} %get-tuple-element.9), channel_id=1, source_target_pairs={{0,64},{16,80},{32,96},{48,112},{64,0},{80,16},{96,32},{112,48},{1... | collective-permute-start | bytes 393224 | tf_op jit(solution)/shard_map/weight_grad/ppermute | solution.py:100
  151.2 3.3 %collective-permute-done.8 = bf16[2,32,1024]{2,1,0:T(8,128)(2,1)} collective-permute-done((bf16[2,32,1024]{2,1,0:T(8,128)(2,1)}, bf16[2,32,1024]{2,1,0:T(8,128)(2,1)}, u32[]{:S(2)}, u32[]{:S(2)}) %collective-permute-start.8) | collective-permute-done | bytes 131104 | tf_op jit(solution)/shard_map/weight_grad/ppermute | solution.py:100
  154.5 6.1 %collective-permute-done.7 = bf16[2,32,1024]{2,1,0:T(8,128)(2,1)} collective-permute-done((bf16[2,32,1024]{2,1,0:T(8,128)(2,1)S(1)}, bf16[2,32,1024]{2,1,0:T(8,128)(2,1)}, u32[]{:S(2)}, u32[]{:S(2)}) %collective-permute-start.7) | collective-permute-done | bytes 131104 | tf_op jit(solution)/shard_map/weight_grad/ppermute | solution.py:100
  160.6 3.7 %collective-permute-done.6 = bf16[2,32,1024]{2,1,0:T(8,128)(2,1)} collective-permute-done((bf16[2,32,1024]{2,1,0:T(8,128)(2,1)S(1)}, bf16[2,32,1024]{2,1,0:T(8,128)(2,1)}, u32[]{:S(2)}, u32[]{:S(2)}) %collective-permute-start.6) | collective-permute-done | bytes 131104 | tf_op jit(solution)/shard_map/weight_grad/ppermute | solution.py:100
  164.3 1.4 fusion.15
  165.7 0.8 broadcast_in_dim.4
  166.5 10.7 %all-to-all-start.2 = ((bf16[6,32,1024]{2,1,0:T(8,128)(2,1)}), bf16[6,32,1024]{2,1,0:T(8,128)(2,1)S(1)}, u32[]{:S(2)}, u32[]{:S(2)}) async-start(bf16[6,32,1024]{2,1,0:T(8,128)(2,1)} %bitcast.70), calls=%async_computation.2 | async-start | bytes 786432 | tf_op jit(solution)/shard_map/weight_grad/all_to_all | solution.py:103
  177.2 1.5 broadcast_select_fusion.1
  179.3 3.7 %fusion.6 = bf16[1024,1024]{1,0:T(8,128)(2,1)} fusion(bf16[1024,1024]{1,0:T(8,128)(2,1)S(1)} %bitcast.67, bf16[512,1024]{1,0:T(8,128)(2,1)S(1)} %get-tuple-element.5, bf16[512,1024]{1,0:T(8,128)(2,1)S(1)} %get-tuple-element.4), kind=kOutput, calls=%fused_computation.15 | convolution fusion | flops 2152726528 | bytes 6291456 | tf_op jit(solution)/shard_map/input_grad/dot_general | solution.py:74
  183.0 10.8 %all-to-all-done.2 = bf16[6,32,1024]{2,1,0:T(8,128)(2,1)S(1)} async-done(((bf16[6,32,1024]{2,1,0:T(8,128)(2,1)}), bf16[6,32,1024]{2,1,0:T(8,128)(2,1)S(1)}, u32[]{:S(2)}, u32[]{:S(2)}) %all-to-all-start.2) | async-done | bytes 393248 | tf_op jit(solution)/shard_map/weight_grad/all_to_all | solution.py:103
  193.8 3.9 %all-to-all-start = ((bf16[8,128,1024]{2,1,0:T(8,128)(2,1)}), bf16[8,128,1024]{2,1,0:T(8,128)(2,1)S(1)}, u32[]{:S(2)}, u32[]{:S(2)}) async-start(bf16[8,128,1024]{2,1,0:T(8,128)(2,1)} %bitcast.68), calls=%async_computation | async-start | bytes 4194304 | tf_op jit(solution)/shard_map/input_grad/all_to_all | solution.py:80
  197.7 26.5 %all-to-all-done = bf16[8,128,1024]{2,1,0:T(8,128)(2,1)S(1)} async-done(((bf16[8,128,1024]{2,1,0:T(8,128)(2,1)}), bf16[8,128,1024]{2,1,0:T(8,128)(2,1)S(1)}, u32[]{:S(2)}, u32[]{:S(2)}) %all-to-all-start) | async-done | bytes 2097184 | tf_op jit(solution)/shard_map/input_grad/all_to_all | solution.py:80
  224.3 1.1 broadcast_in_dim.5
  225.4 10.5 %all-to-all-start.3 = ((bf16[16,32,1024]{2,1,0:T(8,128)(2,1)}), bf16[16,32,1024]{2,1,0:T(8,128)(2,1)S(1)}, u32[]{:S(2)}, u32[]{:S(2)}) async-start(bf16[16,32,1024]{2,1,0:T(8,128)(2,1)} %broadcast_in_dim.5), calls=%async_computation.3 | async-start | bytes 2097152 | tf_op jit(solution)/shard_map/weight_grad/all_to_all | solution.py:108
  235.9 2.7 %reshape.68 = bf16[2,4,128,2,512]{4,3,2,1,0:T(2,128)(2,1)} reshape(bf16[8,128,1024]{2,1,0:T(8,128)(2,1)S(1)} %all-to-all-done) | data formatting | bytes 4194304 | tf_op jit(solution)/shard_map/input_grad/reshape | solution.py:84
  238.6 4.8 %copy.26 = bf16[2,4,128,2,512]{4,0,3,1,2:T(2,128)(2,1)S(1)} copy(bf16[2,4,128,2,512]{4,3,2,1,0:T(2,128)(2,1)} %reshape.68) | data formatting | bytes 4194304 | tf_op jit(solution)/shard_map/input_grad/reshape | solution.py:84
  243.5 2.8 %reshape.69 = bf16[128,8192]{1,0:T(8,128)(2,1)} reshape(bf16[128,4,2,2,512]{4,3,2,1,0:T(2,128)(2,1)S(1)} %bitcast.64) | data formatting | bytes 4194304 | tf_op jit(solution)/shard_map/input_grad/reshape | solution.py:84
  246.3 16.9 %all-to-all-done.3 = bf16[16,32,1024]{2,1,0:T(8,128)(2,1)S(1)} async-done(((bf16[16,32,1024]{2,1,0:T(8,128)(2,1)}), bf16[16,32,1024]{2,1,0:T(8,128)(2,1)S(1)}, u32[]{:S(2)}, u32[]{:S(2)}) %all-to-all-start.3) | async-done | bytes 1048608 | tf_op jit(solution)/shard_map/weight_grad/all_to_all | solution.py:108
  263.1 1.6 bitcast_convert_fusion
  (36 shorter events, 2.2 us)
Async XLA Ops:
  11.9 6.5 %copy-start.7 = (bf16[128,1024]{1,0:T(8,128)(2,1)S(1)}, bf16[128,1024]{1,0:T(8,128)(2,1)}, u32[]{:S(2)}) copy-start(bf16[128,1024]{1,0:T(8,128)(2,1)} %param.5) | copy-start | bytes 786436
  11.9 99.4 %all-to-all-start.1 = ((bf16[16,128,512]{1,2,0:T(8,128)(2,1)}), bf16[16,128,512]{1,2,0:T(8,128)(2,1)}, u32[]{:S(2)}, u32[]{:S(2)}) async-start(bf16[16,128,512]{1,2,0:T(8,128)(2,1)} %bitcast.18), calls=%async_computation.1 | async-start | bytes 4194304 | tf_op jit(solution)/shard_map/inputs/all_to_all | solution.py:70
  18.3 158.9 %all-gather.2.cloned.1.call-start = ((), (), s32[]{:S(2)}) async-start(), calls=%async_computation.4 | async-start | bytes 1179648 | tf_op jit(solution)/shard_map/weight/all_gather | solution.py:49
  18.3 31.7 %collective-permute-start = (bf16[128,1024]{1,0:T(8,128)(2,1)S(1)}, bf16[128,1024]{1,0:T(8,128)(2,1)S(1)}, u32[]{:S(2)}, u32[]{:S(2)}) collective-permute-start(bf16[128,1024]{1,0:T(8,128)(2,1)S(1)} %copy-done.7), channel_id=1, source_target_pairs={{0,128},{128,0},{1,129},{129,1},{2,130},{130,2},{3,131},{131,3},{4... | collective-permute-start | bytes 786440 | tf_op jit(solution)/shard_map/key_grads/ppermute | solution.py:17
  50.2 27.8 %collective-permute-start.1 = (bf16[2,128,1024]{2,1,0:T(8,128)(2,1)S(1)}, bf16[2,128,1024]{2,1,0:T(8,128)(2,1)S(1)}, u32[]{:S(2)}, u32[]{:S(2)}) collective-permute-start(bf16[2,128,1024]{2,1,0:T(8,128)(2,1)S(1)} %pad_maximum_fusion.2), channel_id=1, source_target_pairs={{0,12},{4,8},{8,4},{12,0},{1,13},{5,9},{9,5},{13,1},{2,14},{6,10},... | collective-permute-start | bytes 1572872 | tf_op jit(solution)/shard_map/key_grads/ppermute | solution.py:55
  54.3 23.7 %collective-permute-start.2 = (bf16[2,128,1024]{2,1,0:T(8,128)(2,1)S(1)}, bf16[2,128,1024]{2,1,0:T(8,128)(2,1)S(1)}, u32[]{:S(2)}, u32[]{:S(2)}) collective-permute-start(bf16[2,128,1024]{2,1,0:T(8,128)(2,1)S(1)} %pad_maximum_fusion.2), channel_id=1, source_target_pairs={{0,8},{4,12},{8,0},{12,4},{1,9},{5,13},{9,1},{13,5},{2,10},{6,14},... | collective-permute-start | bytes 1572872 | tf_op jit(solution)/shard_map/key_grads/ppermute | solution.py:55
  57.9 22.6 %collective-permute-start.3 = (bf16[2,128,1024]{2,1,0:T(8,128)(2,1)S(1)}, bf16[2,128,1024]{2,1,0:T(8,128)(2,1)S(1)}, u32[]{:S(2)}, u32[]{:S(2)}) collective-permute-start(bf16[2,128,1024]{2,1,0:T(8,128)(2,1)S(1)} %pad_maximum_fusion.2), channel_id=1, source_target_pairs={{0,4},{4,0},{8,12},{12,8},{1,5},{5,1},{9,13},{13,9},{2,6},{6,2},{1... | collective-permute-start | bytes 1572872 | tf_op jit(solution)/shard_map/key_grads/ppermute | solution.py:55
  80.6 0.8 copy-start.5
  80.8 0.8 copy-start.2
  80.8 1.0 copy-start.3
  80.8 1.1 copy-start.4
  80.8 3.0 %copy-start.10 = (f32[4,1024]{1,0:T(4,128)S(1)}, f32[4,1024]{1,0:T(4,128)}, u32[]{:S(2)}) copy-start(f32[4,1024]{1,0:T(4,128)} %param.7) | copy-start | bytes 49156
  82.0 23.3 %collective-permute-start.4 = (bf16[2,4,128,1024]{3,2,1,0:T(8,128)(2,1)S(1)}, bf16[2,4,128,1024]{3,2,1,0:T(8,128)(2,1)}, u32[]{:S(2)}, u32[]{:S(2)}) collective-permute-start(bf16[2,4,128,1024]{3,2,1,0:T(8,128)(2,1)S(1)} %pad_maximum_fusion.1), channel_id=1, source_target_pairs={{0,1},{1,0},{2,3},{3,2},{4,5},{5,4},{6,7},{7,6},{8,9},{9,8},{10,11... | collective-permute-start | bytes 6291464 | tf_op jit(solution)/shard_map/key_grads/ppermute | solution.py:17
  85.4 19.2 %collective-permute-start.5 = (bf16[64,1024]{1,0:T(8,128)(2,1)S(1)}, bf16[64,1024]{1,0:T(8,128)(2,1)S(1)}, u32[]{:S(2)}, u32[]{:S(2)}) collective-permute-start(bf16[64,1024]{1,0:T(8,128)(2,1)S(1)} %constant_dynamic-slice_fusion), channel_id=1, source_target_pairs={{0,2},{2,0},{1,3},{3,1},{4,6},{6,4},{5,7},{7,5},{8,10},{10,8},{9,1... | collective-permute-start | bytes 393224 | tf_op jit(solution)/shard_map/weight/ppermute | solution.py:17
  104.6 0.7 copy-start.9
  107.6 1.3 copy-start
  120.5 1.0 copy-start.6
  122.2 19.9 %collective-permute-start.12 = (bf16[2,32,1024]{2,1,0:T(8,128)(2,1)S(1)}, bf16[2,32,1024]{2,1,0:T(8,128)(2,1)S(1)}, u32[]{:S(2)}, u32[]{:S(2)}) collective-permute-start(bf16[2,32,1024]{2,1,0:T(8,128)(2,1)S(1)} %get-tuple-element.10), channel_id=1, source_target_pairs={{0,112},{16,0},{32,16},{48,32},{64,48},{80,64},{96,80},{112,96},{1... | collective-permute-start | bytes 393224 | tf_op jit(solution)/shard_map/weight_grad/ppermute | solution.py:100
  126.7 18.7 %collective-permute-start.11 = (bf16[2,32,1024]{2,1,0:T(8,128)(2,1)S(1)}, bf16[2,32,1024]{2,1,0:T(8,128)(2,1)S(1)}, u32[]{:S(2)}, u32[]{:S(2)}) collective-permute-start(bf16[2,32,1024]{2,1,0:T(8,128)(2,1)S(1)} %get-tuple-element.11), channel_id=1, source_target_pairs={{0,16},{16,32},{32,48},{48,64},{64,80},{80,96},{96,112},{112,0},{1... | collective-permute-start | bytes 393224 | tf_op jit(solution)/shard_map/weight_grad/ppermute | solution.py:100
  128.6 22.6 %collective-permute-start.10 = (bf16[2,32,1024]{2,1,0:T(8,128)(2,1)}, bf16[2,32,1024]{2,1,0:T(8,128)(2,1)}, u32[]{:S(2)}, u32[]{:S(2)}) collective-permute-start(bf16[2,32,1024]{2,1,0:T(8,128)(2,1)} %get-tuple-element.12), channel_id=1, source_target_pairs={{0,96},{16,112},{32,0},{48,16},{64,32},{80,48},{96,64},{112,80},{1... | collective-permute-start | bytes 393224 | tf_op jit(solution)/shard_map/weight_grad/ppermute | solution.py:100
  134.5 16.7 %collective-permute-start.9 = (bf16[2,32,1024]{2,1,0:T(8,128)(2,1)}, bf16[2,32,1024]{2,1,0:T(8,128)(2,1)}, u32[]{:S(2)}, u32[]{:S(2)}) collective-permute-start(bf16[2,32,1024]{2,1,0:T(8,128)(2,1)} %get-tuple-element.13), channel_id=1, source_target_pairs={{0,32},{16,48},{32,64},{48,80},{64,96},{80,112},{96,0},{112,16},{1... | collective-permute-start | bytes 393224 | tf_op jit(solution)/shard_map/weight_grad/ppermute | solution.py:100
  136.4 18.1 %collective-permute-start.8 = (bf16[2,32,1024]{2,1,0:T(8,128)(2,1)}, bf16[2,32,1024]{2,1,0:T(8,128)(2,1)}, u32[]{:S(2)}, u32[]{:S(2)}) collective-permute-start(bf16[2,32,1024]{2,1,0:T(8,128)(2,1)} %get-tuple-element.14), channel_id=1, source_target_pairs={{0,80},{16,96},{32,112},{48,0},{64,16},{80,32},{96,48},{112,64},{1... | collective-permute-start | bytes 393224 | tf_op jit(solution)/shard_map/weight_grad/ppermute | solution.py:100
  142.1 18.5 %collective-permute-start.7 = (bf16[2,32,1024]{2,1,0:T(8,128)(2,1)S(1)}, bf16[2,32,1024]{2,1,0:T(8,128)(2,1)}, u32[]{:S(2)}, u32[]{:S(2)}) collective-permute-start(bf16[2,32,1024]{2,1,0:T(8,128)(2,1)S(1)} %get-tuple-element.15), channel_id=1, source_target_pairs={{0,48},{16,64},{32,80},{48,96},{64,112},{80,0},{96,16},{112,32},{1... | collective-permute-start | bytes 393224 | tf_op jit(solution)/shard_map/weight_grad/ppermute | solution.py:100
  145.3 0.7 copy-start.8
  146.0 18.3 %collective-permute-start.6 = (bf16[2,32,1024]{2,1,0:T(8,128)(2,1)S(1)}, bf16[2,32,1024]{2,1,0:T(8,128)(2,1)}, u32[]{:S(2)}, u32[]{:S(2)}) collective-permute-start(bf16[2,32,1024]{2,1,0:T(8,128)(2,1)S(1)} %get-tuple-element.9), channel_id=1, source_target_pairs={{0,64},{16,80},{32,96},{48,112},{64,0},{80,16},{96,32},{112,48},{1... | collective-permute-start | bytes 393224 | tf_op jit(solution)/shard_map/weight_grad/ppermute | solution.py:100
  166.5 27.3 %all-to-all-start.2 = ((bf16[6,32,1024]{2,1,0:T(8,128)(2,1)}), bf16[6,32,1024]{2,1,0:T(8,128)(2,1)S(1)}, u32[]{:S(2)}, u32[]{:S(2)}) async-start(bf16[6,32,1024]{2,1,0:T(8,128)(2,1)} %bitcast.70), calls=%async_computation.2 | async-start | bytes 786432 | tf_op jit(solution)/shard_map/weight_grad/all_to_all | solution.py:103
  177.2 1.9 copy-start.1
  193.8 30.5 %all-to-all-start = ((bf16[8,128,1024]{2,1,0:T(8,128)(2,1)}), bf16[8,128,1024]{2,1,0:T(8,128)(2,1)S(1)}, u32[]{:S(2)}, u32[]{:S(2)}) async-start(bf16[8,128,1024]{2,1,0:T(8,128)(2,1)} %bitcast.68), calls=%async_computation | async-start | bytes 4194304 | tf_op jit(solution)/shard_map/input_grad/all_to_all | solution.py:80
  225.4 37.8 %all-to-all-start.3 = ((bf16[16,32,1024]{2,1,0:T(8,128)(2,1)}), bf16[16,32,1024]{2,1,0:T(8,128)(2,1)S(1)}, u32[]{:S(2)}, u32[]{:S(2)}) async-start(bf16[16,32,1024]{2,1,0:T(8,128)(2,1)} %broadcast_in_dim.5), calls=%async_computation.3 | async-start | bytes 2097152 | tf_op jit(solution)/shard_map/weight_grad/all_to_all | solution.py:108
Sparse Core Ops, SparseCore 0:
  105.4 56.4 all-gather.1

commit v2 on v1

v2 whole, which is shorter than its diff:
```python
import math

import jax
import jax.numpy as jnp
from jax import lax
from jax.experimental import pallas as pl
from jax.experimental.pallas import tpu as pltpu
from jax.experimental.layout import Layout, with_layout_constraint
from jax.sharding import Mesh
from jax.sharding import PartitionSpec as P

QBLOCK = 128
AXES = ("zt", "zp", "yh", "yl", "x", "zh", "c")
SIZES = (3, 2, 2, 4, 4, 2, 2)
BF16 = jnp.bfloat16
F32 = jnp.float32


def swapped(value, axis):
    return lax.ppermute(value, axis, [(0, 1), (1, 0)])


def around_y(value, distance):
    def target(i):
        return (i + (-distance if distance == 2 and i % 2 else distance)) % 8

    return lax.ppermute(value, ("yh", "yl"), [(i, target(i)) for i in range(8)])


def row_major(value):
    return with_layout_constraint(value, Layout(major_to_minor=tuple(range(value.ndim))))


def pack_kernel(source, target):
    nx, half = 4, target.shape[2] // 2
    for x in range(nx):
        for z in range(2):
            for c in range(2):
                for p in range(2):
                    start = (((x * 2 + z) * 2 + c) * 2 + p) * half
                    slot = (c * 2 + p) * nx + x
                    target[slot, :, z * half : (z + 1) * half] = source[:, start : start + half]


def packed(inputs):
    tokens, width = inputs.shape
    block = tokens // 4
    return pl.pallas_call(
        pack_kernel,
        grid=(tokens // block,),
        out_shape=jax.ShapeDtypeStruct((16, tokens, width // 16), inputs.dtype),
        in_specs=[pl.BlockSpec((block, width), lambda i: (i, 0))],
        out_specs=pl.BlockSpec((16, block, width // 16), lambda i: (0, i, 0)),
        cost_estimate=pl.CostEstimate(
            flops=0, bytes_accessed=4 * tokens * width, transcendentals=0
        ),
    )(inputs)


def pair_in_order(mine, other, position, axis):
    first = jnp.where(position == 0, mine, other)
    second = jnp.where(position == 0, other, mine)
    return jnp.concatenate([first, second], axis=axis)


def local(inputs, key_grad, weight_codes, weight_scales):
    tokens, width = inputs.shape
    rows, cols = weight_codes.shape
    scale_rows = weight_scales.shape[0]
    zp, yh, yl, x, zh, c = (
        lax.axis_index(a) for a in ("zp", "yh", "yl", "x", "zh", "c")
    )
    nx, ny, nt = 4, 8, 3
    half = rows // 2
    piece = half // ny
    y = yh * 4 + yl
    total_tokens = tokens * math.prod(SIZES)
    factor = 1.0 / math.sqrt(total_tokens)

    with jax.named_scope("weight"):
        weight = (
            (
                weight_codes.astype(F32).reshape(scale_rows, QBLOCK, cols)
                * weight_scales[:, None, :]
            )
            .reshape(rows, cols)
            .astype(BF16)
        )
        share = rows // ny
        mine = lax.dynamic_slice_in_dim(weight, y * share, share, 0)

    with jax.named_scope("inputs"):
        theirs = swapped(mine, "zh")
        key_other = swapped(key_grad, "zp")

    with jax.named_scope("key_grads"):
        both = pair_in_order(key_grad[None], key_other[None], zp, 0)
        both, theirs = lax.optimization_barrier((both, theirs))
        shares = pair_in_order(theirs[None], swapped(theirs, "yh")[None], yh, 0)
        from_left = lax.ppermute(both, "x", [(i, (i + 1) % nx) for i in range(nx)])
        from_right = lax.ppermute(both, "x", [(i, (i - 1) % nx) for i in range(nx)])
        opposite = lax.ppermute(from_right, "x", [(i, (i - 1) % nx) for i in range(nx)])
        sent, from_left, opposite, shares = lax.optimization_barrier(
            (packed(inputs), from_left, opposite, shares)
        )
        by_distance = [both, from_right, opposite, from_left]
        slots = []
        for i in range(nx):
            value = by_distance[0]
            for k in range(1, nx):
                value = jnp.where((x + k) % nx == i, by_distance[k], value)
            slots.append(value)
        column = jnp.stack(slots, axis=1)
        keys = pair_in_order(column[None], swapped(column, "c")[None], c, 0)

    with jax.named_scope("inputs"):
        got = row_major(lax.all_to_all(sent, ("c", "zp", "x"), 0, 0, tiled=True))

    with jax.named_scope("input_grad"):
        near = [shares] + [around_y(shares, distance) for distance in (-1, 2, 1)]
        slots = []
        for i in range(4):
            value = near[0]
            for k in (1, 2, 3):
                value = jnp.where((yl + k) % 4 == i, near[k], value)
            slots.append(value)
        weight_other = jnp.stack(slots, axis=1).reshape(rows, cols)
        weights = pair_in_order(weight, weight_other, zh, 0)
        own = lax.dynamic_index_in_dim(keys, zp, 1, keepdims=False)
        local_part = lax.dot_general(
            own.reshape(2 * nx * tokens, cols),
            weights,
            (((1,), (1,)), ((), ())),
            preferred_element_type=F32,
        ).astype(BF16)
        got, local_part = lax.optimization_barrier((got, local_part))
        back = lax.all_to_all(
            local_part.reshape(2 * nx, tokens, 2 * rows), ("c", "x"), 0, 0, tiled=True
        )

    with jax.named_scope("weight_grad"):
        partial_value = lax.dot_general(
            got.reshape(4 * nx * tokens, 2 * half),
            keys.reshape(4 * nx * tokens, cols),
            (((0,), (0,)), ((), ())),
            preferred_element_type=F32,
        ) * factor
        chunks = row_major(partial_value.astype(BF16)).reshape(2, 2, 4, piece, cols)
        total = lax.dynamic_index_in_dim(chunks, yl, 2, keepdims=False).astype(F32)
        for k in (2, 1, 3):
            out = lax.dynamic_index_in_dim(chunks, (yl + k) % 4, 2, keepdims=False)
            total = total + around_y(out, -1 if k == 3 else k).astype(F32)
        kept = lax.dynamic_index_in_dim(total, yh, 1, keepdims=False)
        given = lax.dynamic_index_in_dim(total, 1 - yh, 1, keepdims=False).astype(BF16)
        total = (kept + swapped(given, "yh").astype(F32)).astype(BF16)
        total, back = lax.optimization_barrier((total, back))
        spread = jnp.broadcast_to(total[None], (nt, 2, piece, cols))
        spread = lax.all_to_all(
            spread.reshape(2 * nt, piece, cols), ("zt", "zh"), 0, 0, tiled=True
        )
        summed = spread.astype(F32).sum(axis=0).astype(BF16)
        spread = jnp.broadcast_to(summed[None], (2 * ny, piece, cols))
        gathered = lax.all_to_all(spread, ("zp", "yh", "yl"), 0, 0, tiled=True)
        weight_grad = gathered.reshape(rows, cols).astype(F32)

    with jax.named_scope("input_grad"):
        input_grad = (
            back.reshape(2, nx, tokens, 2, rows).transpose(2, 1, 3, 0, 4).reshape(tokens, width)
        )
    return (input_grad, weight_grad)


def solution(mesh):
    fine = Mesh(mesh.devices.reshape(SIZES), AXES)
    tokens_over = P(AXES, None)
    rows_over = P(("x", "zh", "c"), None)
    return jax.shard_map(
        local,
        mesh=fine,
        in_specs=(tokens_over, tokens_over, rows_over, rows_over),
        out_specs=(tokens_over, rows_over),
        check_vma=False,
    )
```

time: 273 us -> 213 us (0.78)
  waiting for transfers between devices: 120 us -> 51.1 us
  blocking collectives: 0 us -> 30.6 us
  between operations: 14.5 us -> 1.19 us
  local copies, waits for them, and re-layouts: 26.5 us -> 17.5 us
  Pallas kernels: 0 us -> 3.78 us
    all_to_all x0 -> x1, blocking collectives: none -> 30.6 us  [local(): lax.all_to_all(spread.reshape(2 * nt, piece, cols), ('zt', 'zh'), 0, 0, t...]
    all_to_all x1, waiting for transfers between devices: 26.5 us -> 0.01 us  [local(): lax.all_to_all(local_part.reshape(2 * nx, tokens, 2 * rows), ('c', 'x'),...]
    ppermute x3 -> x5, waiting for transfers between devices: 32.2 us -> 12 us  [swapped(): return lax.ppermute(value, axis, [(0, 1), (1, 0)])]
    all_to_all x3 -> x2, waiting for transfers between devices: 27.7 us -> 11.9 us  [the longest x1 11.9 us: local(): gathered = lax.all_to_all(spread, ('zp', 'yh', 'yl'), 0, 0, tiled=True)]
    ppermute x3 -> x5, starting transfers between devices: 20.5 us -> 32.9 us  [swapped(): return lax.ppermute(value, axis, [(0, 1), (1, 0)])]
    all_to_all x3 -> x2, starting transfers between devices: 27.6 us -> 16 us  [the longest x1 11.6 us: local(): gathered = lax.all_to_all(spread, ('zp', 'yh', 'yl'), 0, 0, tiled=True)]
    ppermute x10 -> x9, waiting for transfers between devices: 33.6 us -> 27.2 us  [the longest x6 19 us: around_y(): return lax.ppermute(value, ('yh', 'yl'), [(i, target(i)) for i in range(8)])]
    unnamed x23 -> x24, local copies, waits for them, and re-layouts: 8.04 us -> 3.81 us
  transfers between devices with their start and end apart: 18 -> 17, of which waited for: 10 -> 10; matrix products, arithmetic and copies ran while one was open for 13% -> 15% of each run, Pallas kernels for 0% -> 2%
where the time goes in v2:
time: 213 us; the launch traced here: 212 us
  starting transfers between devices  87.6 us (41%)
  waiting for transfers between devices  51.1 us (24%)
  blocking collectives  30.6 us (14%)
  local copies, waits for them, and re-layouts  17.5 us (8%)
  other arithmetic  12.4 us (6%)
  matrix products  7.63 us (4%)
  Pallas kernels  3.78 us (2%)
    ppermute x5, starting transfers between devices, swapped(): return lax.ppermute(value, axis, [(0, 1), (1, 0)])  32.9 us
    all_to_all x1, blocking collectives, local(): lax.all_to_all(spread.reshape(2 * nt, piece, cols), ('zt', 'zh'), 0, 0, t...  30.6 us
    ppermute x6, starting transfers between devices, around_y(): return lax.ppermute(value, ('yh', 'yl'), [(i, target(i)) for i in range(8)])  22 us
    ppermute x6, waiting for transfers between devices, around_y(): return lax.ppermute(value, ('yh', 'yl'), [(i, target(i)) for i in range(8)])  19 us
    reshape x3, local copies, waits for them, and re-layouts, local(): back.reshape(2, nx, tokens, 2, rows).transpose(2, 1, 3, 0, 4)  12.3 us
    ppermute x5, waiting for transfers between devices, swapped(): return lax.ppermute(value, axis, [(0, 1), (1, 0)])  12 us
    all_to_all x1, waiting for transfers between devices, local(): gathered = lax.all_to_all(spread, ('zp', 'yh', 'yl'), 0, 0, tiled=True)  11.9 us
    all_to_all x1, starting transfers between devices, local(): gathered = lax.all_to_all(spread, ('zp', 'yh', 'yl'), 0, 0, tiled=True)  11.6 us
  transfers between devices with their start and end apart: 17, of which 10 were waited for; matrix products, arithmetic and copies ran while one was open for 15% of the time, Pallas kernels for 2%

profile of v2, /device:TPU:8, one launch (start us, length us, event | category | flops | bytes accessed | tf_op | source)
XLA Modules:
  0.0 211.8 jit_solution(6473971167110618669)
XLA Ops:
  0.6 4.4 %collective-permute-start = (bf16[128,1024]{1,0:T(8,128)(2,1)}, bf16[128,1024]{1,0:T(8,128)(2,1)S(1)}, u32[]{:S(2)}, u32[]{:S(2)}) collective-permute-start(bf16[128,1024]{1,0:T(8,128)(2,1)} %param.5), channel_id=1, source_target_pairs={{0,128},{128,0},{1,129},{129,1},{2,130},{130,2},{3,131},{131,3},{4... | collective-permute-start | bytes 786440 | tf_op jit(solution)/shard_map/inputs/ppermute | solution.py:20
  5.1 1.5 fusion.5
  6.6 14.8 %collective-permute-start.1 = (bf16[64,1024]{1,0:T(8,128)(2,1)S(1)}, bf16[64,1024]{1,0:T(8,128)(2,1)S(1)}, u32[]{:S(2)}, u32[]{:S(2)}) collective-permute-start(bf16[64,1024]{1,0:T(8,128)(2,1)S(1)} %constant_dynamic-slice_fusion), channel_id=1, source_target_pairs={{0,2},{2,0},{1,3},{3,1},{4,6},{6,4},{5,7},{7,5},{8,10},{10,8},{9,1... | collective-permute-start | bytes 393224 | tf_op jit(solution)/shard_map/inputs/ppermute | solution.py:20
  21.6 5.5 %collective-permute-done.1 = bf16[64,1024]{1,0:T(8,128)(2,1)S(1)} collective-permute-done((bf16[64,1024]{1,0:T(8,128)(2,1)S(1)}, bf16[64,1024]{1,0:T(8,128)(2,1)S(1)}, u32[]{:S(2)}, u32[]{:S(2)}) %collective-permute-start.1) | collective-permute-done | bytes 131104 | tf_op jit(solution)/shard_map/inputs/ppermute | solution.py:20
  27.1 4.7 %collective-permute-start.3 = (bf16[2,128,1024]{2,1,0:T(8,128)(2,1)S(1)}, bf16[2,128,1024]{2,1,0:T(8,128)(2,1)S(1)}, u32[]{:S(2)}, u32[]{:S(2)}) collective-permute-start(bf16[2,128,1024]{2,1,0:T(8,128)(2,1)S(1)} %pad_maximum_fusion.3), channel_id=1, source_target_pairs={{0,12},{4,0},{8,4},{12,8},{1,13},{5,1},{9,5},{13,9},{2,14},{6,2},{... | collective-permute-start | bytes 1572872 | tf_op jit(solution)/shard_map/key_grads/ppermute | solution.py:101
  31.8 1.9 collective-permute-start.2
  33.7 8.3 %collective-permute-done.3 = bf16[2,128,1024]{2,1,0:T(8,128)(2,1)S(1)} collective-permute-done((bf16[2,128,1024]{2,1,0:T(8,128)(2,1)S(1)}, bf16[2,128,1024]{2,1,0:T(8,128)(2,1)S(1)}, u32[]{:S(2)}, u32[]{:S(2)}) %collective-permute-start.3) | collective-permute-done | bytes 524320 | tf_op jit(solution)/shard_map/key_grads/ppermute | solution.py:101
  42.0 5.6 %collective-permute-start.4 = (bf16[2,128,1024]{2,1,0:T(8,128)(2,1)S(1)}, bf16[2,128,1024]{2,1,0:T(8,128)(2,1)S(1)}, u32[]{:S(2)}, u32[]{:S(2)}) collective-permute-start(bf16[2,128,1024]{2,1,0:T(8,128)(2,1)S(1)} %collective-permute-done.3), channel_id=1, source_target_pairs={{0,12},{4,0},{8,4},{12,8},{1,13},{5,1},{9,5},{13,9},{2,14},{6,2},{... | collective-permute-start | bytes 1572872 | tf_op jit(solution)/shard_map/key_grads/ppermute | solution.py:102
  47.6 6.8 %collective-permute-start.5 = (bf16[64,1024]{1,0:T(8,128)(2,1)S(1)}, bf16[64,1024]{1,0:T(8,128)(2,1)S(1)}, u32[]{:S(2)}, u32[]{:S(2)}) collective-permute-start(bf16[64,1024]{1,0:T(8,128)(2,1)S(1)} %collective-permute-done.1), channel_id=1, source_target_pairs={{0,64},{64,0},{1,65},{65,1},{2,66},{66,2},{3,67},{67,3},{4,68},{68... | collective-permute-start | bytes 393224 | tf_op jit(solution)/shard_map/key_grads/ppermute | solution.py:20
  54.4 3.8 %key_grads.1 = bf16[16,128,512]{2,1,0:T(8,128)(2,1)} custom-call(bf16[128,8192]{1,0:T(8,128)(2,1)} %source.1), custom_call_target="tpu_custom_call" | custom-call | bytes 4194304 | tf_op jit(solution)/shard_map/key_grads/pallas_call | solution.py:48
  58.2 0.4 collective-permute-done.5
  58.7 0.8 copy-done.7
  59.4 0.2 copy-done.8
  59.6 4.4 %all-to-all-start = ((bf16[16,128,512]{2,1,0:T(8,128)(2,1)}), bf16[16,128,512]{2,1,0:T(8,128)(2,1)}, u32[]{:S(2)}, u32[]{:S(2)}) async-start(bf16[16,128,512]{2,1,0:T(8,128)(2,1)} %key_grads.1), calls=%async_computation | async-start | bytes 4194304 | tf_op jit(solution)/shard_map/inputs/all_to_all | solution.py:117
  64.1 1.8 select_bitcast_fusion.5
  65.9 1.6 pad_maximum_fusion.1
  67.5 2.1 %collective-permute-start.6 = (bf16[2,4,128,1024]{3,2,1,0:T(8,128)(2,1)}, bf16[2,4,128,1024]{3,2,1,0:T(8,128)(2,1)}, u32[]{:S(2)}, u32[]{:S(2)}) collective-permute-start(bf16[2,4,128,1024]{3,2,1,0:T(8,128)(2,1)} %pad_maximum_fusion.1), channel_id=1, source_target_pairs={{0,1},{1,0},{2,3},{3,2},{4,5},{5,4},{6,7},{7,6},{8,9},{9,8},{10,11... | collective-permute-start | bytes 6291464 | tf_op jit(solution)/shard_map/key_grads/ppermute | solution.py:20
  69.7 3.6 %collective-permute-start.7 = (bf16[2,64,1024]{2,1,0:T(8,128)(2,1)S(1)}, bf16[2,64,1024]{2,1,0:T(8,128)(2,1)S(1)}, u32[]{:S(2)}, u32[]{:S(2)}) collective-permute-start(bf16[2,64,1024]{2,1,0:T(8,128)(2,1)S(1)} %pad_maximum_fusion.4), channel_id=1, source_target_pairs={{0,16},{16,32},{32,48},{48,64},{64,80},{80,96},{96,112},{112,0},{1... | collective-permute-start | bytes 786440 | tf_op jit(solution)/shard_map/input_grad/ppermute | solution.py:27
  73.3 4.8 %collective-permute-start.8 = (bf16[2,64,1024]{2,1,0:T(8,128)(2,1)S(1)}, bf16[2,64,1024]{2,1,0:T(8,128)(2,1)S(1)}, u32[]{:S(2)}, u32[]{:S(2)}) collective-permute-start(bf16[2,64,1024]{2,1,0:T(8,128)(2,1)S(1)} %pad_maximum_fusion.4), channel_id=1, source_target_pairs={{0,32},{16,112},{32,64},{48,16},{64,96},{80,48},{96,0},{112,80},{1... | collective-permute-start | bytes 786440 | tf_op jit(solution)/shard_map/input_grad/ppermute | solution.py:27
  78.1 2.5 %collective-permute-start.9 = (bf16[2,64,1024]{2,1,0:T(8,128)(2,1)S(1)}, bf16[2,64,1024]{2,1,0:T(8,128)(2,1)}, u32[]{:S(2)}, u32[]{:S(2)}) collective-permute-start(bf16[2,64,1024]{2,1,0:T(8,128)(2,1)S(1)} %pad_maximum_fusion.4), channel_id=1, source_target_pairs={{0,112},{16,0},{32,16},{48,32},{64,48},{80,64},{96,80},{112,96},{1... | collective-permute-start | bytes 786440 | tf_op jit(solution)/shard_map/input_grad/ppermute | solution.py:27
  80.7 6.5 %collective-permute-done.8 = bf16[2,64,1024]{2,1,0:T(8,128)(2,1)S(1)} collective-permute-done((bf16[2,64,1024]{2,1,0:T(8,128)(2,1)S(1)}, bf16[2,64,1024]{2,1,0:T(8,128)(2,1)S(1)}, u32[]{:S(2)}, u32[]{:S(2)}) %collective-permute-start.8) | collective-permute-done | bytes 262176 | tf_op jit(solution)/shard_map/input_grad/ppermute | solution.py:27
  87.2 0.7 copy-done.10
  87.9 4.3 %collective-permute-done.9 = bf16[2,64,1024]{2,1,0:T(8,128)(2,1)} collective-permute-done((bf16[2,64,1024]{2,1,0:T(8,128)(2,1)S(1)}, bf16[2,64,1024]{2,1,0:T(8,128)(2,1)}, u32[]{:S(2)}, u32[]{:S(2)}) %collective-permute-start.9) | collective-permute-done | bytes 262176 | tf_op jit(solution)/shard_map/input_grad/ppermute | solution.py:27
  92.2 1.2 select_bitcast_fusion.9
  93.7 0.2 bitcast_select_fusion.1
  93.9 0.8 copy-done.2
  94.9 1.8 select_bitcast_fusion
  96.7 0.2 fusion
  96.9 1.2 copy-done
  98.1 3.7 %fusion.6 = bf16[1024,1024]{1,0:T(8,128)(2,1)} fusion(bf16[1024,1024]{1,0:T(8,128)(2,1)S(1)} %bitcast.73, bf16[512,1024]{1,0:T(8,128)(2,1)S(1)} %get-tuple-element.25, bf16[512,1024]{1,0:T(8,128)(2,1)S(1)} %get-tuple-element.24), kind=kOutput, calls=%fused_computation.15 | convolution fusion | flops 2152726528 | bytes 6291456 | tf_op jit(solution)/shard_map/input_grad/dot_general | solution.py:130
  101.8 4.5 %all-to-all-start.1 = ((bf16[8,128,1024]{2,1,0:T(8,128)(2,1)}), bf16[8,128,1024]{2,1,0:T(8,128)(2,1)}, u32[]{:S(2)}, u32[]{:S(2)}) async-start(bf16[8,128,1024]{2,1,0:T(8,128)(2,1)} %bitcast.74), calls=%async_computation.1 | async-start | bytes 4194304 | tf_op jit(solution)/shard_map/input_grad/all_to_all | solution.py:137
  106.2 2.0 pad_maximum_fusion
  108.2 3.9 %multiply_convert_fusion = bf16[512,1024]{1,0:T(8,128)(2,1)S(1)} fusion(bf16[2048,512]{1,0:T(8,128)(2,1)} %bitcast.20, bf16[2048,1024]{1,0:T(8,128)(2,1)S(1)} %bitcast.72), kind=kOutput, calls=%fused_computation.12 | convolution fusion | flops 2148532224 | bytes 7340032 | tf_op jit(solution)/shard_map/weight_grad/dot_general | solution.py:142
  112.2 2.0 collective-permute-start.12
  114.2 3.9 %collective-permute-start.11 = (bf16[2,2,32,1024]{3,2,1,0:T(8,128)(2,1)S(1)}, bf16[2,2,32,1024]{3,2,1,0:T(8,128)(2,1)S(1)}, u32[]{:S(2)}, u32[]{:S(2)}) collective-permute-start(bf16[2,2,32,1024]{3,2,1,0:T(8,128)(2,1)S(1)} %get-tuple-element.32), channel_id=1, source_target_pairs={{0,16},{16,32},{32,48},{48,64},{64,80},{80,96},{96,112},{112,0},{1... | collective-permute-start | bytes 786440 | tf_op jit(solution)/shard_map/weight_grad/ppermute | solution.py:27
  118.1 5.3 %collective-permute-start.10 = (bf16[2,2,32,1024]{3,2,1,0:T(8,128)(2,1)S(1)}, bf16[2,2,32,1024]{3,2,1,0:T(8,128)(2,1)S(1)}, u32[]{:S(2)}, u32[]{:S(2)}) collective-permute-start(bf16[2,2,32,1024]{3,2,1,0:T(8,128)(2,1)S(1)} %get-tuple-element.30), channel_id=1, source_target_pairs={{0,32},{16,112},{32,64},{48,16},{64,96},{80,48},{96,0},{112,80},{1... | collective-permute-start | bytes 786440 | tf_op jit(solution)/shard_map/weight_grad/ppermute | solution.py:27
  123.4 2.5 %collective-permute-done.11 = bf16[2,2,32,1024]{3,2,1,0:T(8,128)(2,1)S(1)} collective-permute-done((bf16[2,2,32,1024]{3,2,1,0:T(8,128)(2,1)S(1)}, bf16[2,2,32,1024]{3,2,1,0:T(8,128)(2,1)S(1)}, u32[]{:S(2)}, u32[]{:S(2)}) %collective-permute-start.11) | collective-permute-done | bytes 262176 | tf_op jit(solution)/shard_map/weight_grad/ppermute | solution.py:27
  125.8 5.6 %collective-permute-done.10 = bf16[2,2,32,1024]{3,2,1,0:T(8,128)(2,1)S(1)} collective-permute-done((bf16[2,2,32,1024]{3,2,1,0:T(8,128)(2,1)S(1)}, bf16[2,2,32,1024]{3,2,1,0:T(8,128)(2,1)S(1)}, u32[]{:S(2)}, u32[]{:S(2)}) %collective-permute-start.10) | collective-permute-done | bytes 262176 | tf_op jit(solution)/shard_map/weight_grad/ppermute | solution.py:27
  131.7 4.7 %collective-permute-start.13 = (bf16[2,32,1024]{2,1,0:T(8,128)(2,1)S(1)}, bf16[2,32,1024]{2,1,0:T(8,128)(2,1)S(1)}, u32[]{:S(2)}, u32[]{:S(2)}) collective-permute-start(bf16[2,32,1024]{2,1,0:T(8,128)(2,1)S(1)} %fusion.12), channel_id=1, source_target_pairs={{0,64},{64,0},{1,65},{65,1},{2,66},{66,2},{3,67},{67,3},{4,68},{68... | collective-permute-start | bytes 393224 | tf_op jit(solution)/shard_map/weight_grad/ppermute | solution.py:20
  136.4 6.1 %collective-permute-done.13 = bf16[2,32,1024]{2,1,0:T(8,128)(2,1)S(1)} collective-permute-done((bf16[2,32,1024]{2,1,0:T(8,128)(2,1)S(1)}, bf16[2,32,1024]{2,1,0:T(8,128)(2,1)S(1)}, u32[]{:S(2)}, u32[]{:S(2)}) %collective-permute-start.13) | collective-permute-done | bytes 131104 | tf_op jit(solution)/shard_map/weight_grad/ppermute | solution.py:20
  142.6 30.6 %all_to_all.20 = bf16[6,32,1024]{2,1,0:T(8,128)(2,1)S(1)} all-to-all(bf16[6,32,1024]{2,1,0:T(8,128)(2,1)S(1)} %bitcast.75), channel_id=1, replica_groups=mesh['zt'=3,'zp'=2,'yh'=2,'yl'=4,'x'=4,'zh'=2,'c'=2] {'zt','zh'}, dimensions={0} | all-to-all | bytes 786432 | tf_op jit(solution)/shard_map/weight_grad/all_to_all | solution.py:158
  173.3 1.1 broadcast_in_dim.5
  174.4 11.6 %all-to-all-start.3 = ((bf16[16,32,1024]{2,1,0:T(8,128)(2,1)}), bf16[16,32,1024]{2,1,0:T(8,128)(2,1)S(1)}, u32[]{:S(2)}, u32[]{:S(2)}) async-start(bf16[16,32,1024]{2,1,0:T(8,128)(2,1)} %broadcast_in_dim.5), calls=%async_computation.3 | async-start | bytes 2097152 | tf_op jit(solution)/shard_map/weight_grad/all_to_all | solution.py:163
  185.9 3.3 %reshape.56 = bf16[2,4,128,2,512]{4,3,2,1,0:T(2,128)(2,1)S(1)} reshape(bf16[8,128,1024]{2,1,0:T(8,128)(2,1)} %all-to-all-done.1) | data formatting | bytes 4194304 | tf_op jit(solution)/shard_map/input_grad/reshape | solution.py:168
  189.2 4.6 %copy.19 = bf16[2,4,128,2,512]{4,0,3,1,2:T(2,128)(2,1)} copy(bf16[2,4,128,2,512]{4,3,2,1,0:T(2,128)(2,1)S(1)} %reshape.56) | data formatting | bytes 4194304 | tf_op jit(solution)/shard_map/input_grad/reshape | solution.py:168
  193.8 4.5 %reshape.57 = bf16[128,8192]{1,0:T(8,128)(2,1)} reshape(bf16[128,4,2,2,512]{4,3,2,1,0:T(2,128)(2,1)} %bitcast.71) | data formatting | bytes 4194304 | tf_op jit(solution)/shard_map/input_grad/reshape | solution.py:168
  198.3 11.9 %all-to-all-done.3 = bf16[16,32,1024]{2,1,0:T(8,128)(2,1)S(1)} async-done(((bf16[16,32,1024]{2,1,0:T(8,128)(2,1)}), bf16[16,32,1024]{2,1,0:T(8,128)(2,1)S(1)}, u32[]{:S(2)}, u32[]{:S(2)}) %all-to-all-start.3) | async-done | bytes 1048608 | tf_op jit(solution)/shard_map/weight_grad/all_to_all | solution.py:163
  210.1 1.6 bitcast_convert_fusion
  (40 shorter events, 1.0 us)
Async XLA Ops:
  0.6 20.8 %copy-start.11 = (bf16[128,1024]{1,0:T(8,128)(2,1)S(1)}, bf16[128,1024]{1,0:T(8,128)(2,1)}, u32[]{:S(2)}) copy-start(bf16[128,1024]{1,0:T(8,128)(2,1)} %param.5) | copy-start | bytes 786436
  0.6 20.8 %collective-permute-start = (bf16[128,1024]{1,0:T(8,128)(2,1)}, bf16[128,1024]{1,0:T(8,128)(2,1)S(1)}, u32[]{:S(2)}, u32[]{:S(2)}) collective-permute-start(bf16[128,1024]{1,0:T(8,128)(2,1)} %param.5), channel_id=1, source_target_pairs={{0,128},{128,0},{1,129},{129,1},{2,130},{130,2},{3,131},{131,3},{4... | collective-permute-start | bytes 786440 | tf_op jit(solution)/shard_map/inputs/ppermute | solution.py:20
  6.6 20.5 %collective-permute-start.1 = (bf16[64,1024]{1,0:T(8,128)(2,1)S(1)}, bf16[64,1024]{1,0:T(8,128)(2,1)S(1)}, u32[]{:S(2)}, u32[]{:S(2)}) collective-permute-start(bf16[64,1024]{1,0:T(8,128)(2,1)S(1)} %constant_dynamic-slice_fusion), channel_id=1, source_target_pairs={{0,2},{2,0},{1,3},{3,1},{4,6},{6,4},{5,7},{7,5},{8,10},{10,8},{9,1... | collective-permute-start | bytes 393224 | tf_op jit(solution)/shard_map/inputs/ppermute | solution.py:20
  21.6 42.5 %copy-start.5 = (bf16[2,128,1024]{2,1,0:T(8,128)(2,1)}, bf16[2,128,1024]{2,1,0:T(8,128)(2,1)S(1)}, u32[]{:S(2)}) copy-start(bf16[2,128,1024]{2,1,0:T(8,128)(2,1)S(1)} %pad_maximum_fusion.3) | copy-start | bytes 1572868
  27.1 14.8 %collective-permute-start.3 = (bf16[2,128,1024]{2,1,0:T(8,128)(2,1)S(1)}, bf16[2,128,1024]{2,1,0:T(8,128)(2,1)S(1)}, u32[]{:S(2)}, u32[]{:S(2)}) collective-permute-start(bf16[2,128,1024]{2,1,0:T(8,128)(2,1)S(1)} %pad_maximum_fusion.3), channel_id=1, source_target_pairs={{0,12},{4,0},{8,4},{12,8},{1,13},{5,1},{9,5},{13,9},{2,14},{6,2},{... | collective-permute-start | bytes 1572872 | tf_op jit(solution)/shard_map/key_grads/ppermute | solution.py:101
  31.8 26.8 %collective-permute-start.2 = (bf16[2,128,1024]{2,1,0:T(8,128)(2,1)S(1)}, bf16[2,128,1024]{2,1,0:T(8,128)(2,1)S(1)}, u32[]{:S(2)}, u32[]{:S(2)}) collective-permute-start(bf16[2,128,1024]{2,1,0:T(8,128)(2,1)S(1)} %pad_maximum_fusion.3), channel_id=1, source_target_pairs={{0,4},{4,8},{8,12},{12,0},{1,5},{5,9},{9,13},{13,1},{2,6},{6,10},{... | collective-permute-start | bytes 1572872 | tf_op jit(solution)/shard_map/key_grads/ppermute | solution.py:100
  42.0 16.2 %copy-start.6 = (bf16[2,128,1024]{2,1,0:T(8,128)(2,1)}, bf16[2,128,1024]{2,1,0:T(8,128)(2,1)S(1)}, u32[]{:S(2)}) copy-start(bf16[2,128,1024]{2,1,0:T(8,128)(2,1)S(1)} %collective-permute-done.3) | copy-start | bytes 1572868
  42.0 16.7 %collective-permute-start.4 = (bf16[2,128,1024]{2,1,0:T(8,128)(2,1)S(1)}, bf16[2,128,1024]{2,1,0:T(8,128)(2,1)S(1)}, u32[]{:S(2)}, u32[]{:S(2)}) collective-permute-start(bf16[2,128,1024]{2,1,0:T(8,128)(2,1)S(1)} %collective-permute-done.3), channel_id=1, source_target_pairs={{0,12},{4,0},{8,4},{12,8},{1,13},{5,1},{9,5},{13,9},{2,14},{6,2},{... | collective-permute-start | bytes 1572872 | tf_op jit(solution)/shard_map/key_grads/ppermute | solution.py:102
  47.6 11.0 %collective-permute-start.5 = (bf16[64,1024]{1,0:T(8,128)(2,1)S(1)}, bf16[64,1024]{1,0:T(8,128)(2,1)S(1)}, u32[]{:S(2)}, u32[]{:S(2)}) collective-permute-start(bf16[64,1024]{1,0:T(8,128)(2,1)S(1)} %collective-permute-done.1), channel_id=1, source_target_pairs={{0,64},{64,0},{1,65},{65,1},{2,66},{66,2},{3,67},{67,3},{4,68},{68... | collective-permute-start | bytes 393224 | tf_op jit(solution)/shard_map/key_grads/ppermute | solution.py:20
  58.6 0.8 copy-start.7
  58.6 1.0 copy-start.8
  59.6 42.2 %all-to-all-start = ((bf16[16,128,512]{2,1,0:T(8,128)(2,1)}), bf16[16,128,512]{2,1,0:T(8,128)(2,1)}, u32[]{:S(2)}, u32[]{:S(2)}) async-start(bf16[16,128,512]{2,1,0:T(8,128)(2,1)} %key_grads.1), calls=%async_computation | async-start | bytes 4194304 | tf_op jit(solution)/shard_map/inputs/all_to_all | solution.py:117
  65.9 1.7 copy-start.1
  65.9 1.7 copy-start.3
  67.5 26.4 %collective-permute-start.6 = (bf16[2,4,128,1024]{3,2,1,0:T(8,128)(2,1)}, bf16[2,4,128,1024]{3,2,1,0:T(8,128)(2,1)}, u32[]{:S(2)}, u32[]{:S(2)}) collective-permute-start(bf16[2,4,128,1024]{3,2,1,0:T(8,128)(2,1)} %pad_maximum_fusion.1), channel_id=1, source_target_pairs={{0,1},{1,0},{2,3},{3,2},{4,5},{5,4},{6,7},{7,6},{8,9},{9,8},{10,11... | collective-permute-start | bytes 6291464 | tf_op jit(solution)/shard_map/key_grads/ppermute | solution.py:20
  69.7 11.0 %collective-permute-start.7 = (bf16[2,64,1024]{2,1,0:T(8,128)(2,1)S(1)}, bf16[2,64,1024]{2,1,0:T(8,128)(2,1)S(1)}, u32[]{:S(2)}, u32[]{:S(2)}) collective-permute-start(bf16[2,64,1024]{2,1,0:T(8,128)(2,1)S(1)} %pad_maximum_fusion.4), channel_id=1, source_target_pairs={{0,16},{16,32},{32,48},{48,64},{64,80},{80,96},{96,112},{112,0},{1... | collective-permute-start | bytes 786440 | tf_op jit(solution)/shard_map/input_grad/ppermute | solution.py:27
  73.3 13.9 %collective-permute-start.8 = (bf16[2,64,1024]{2,1,0:T(8,128)(2,1)S(1)}, bf16[2,64,1024]{2,1,0:T(8,128)(2,1)S(1)}, u32[]{:S(2)}, u32[]{:S(2)}) collective-permute-start(bf16[2,64,1024]{2,1,0:T(8,128)(2,1)S(1)} %pad_maximum_fusion.4), channel_id=1, source_target_pairs={{0,32},{16,112},{32,64},{48,16},{64,96},{80,48},{96,0},{112,80},{1... | collective-permute-start | bytes 786440 | tf_op jit(solution)/shard_map/input_grad/ppermute | solution.py:27
  78.1 14.2 %collective-permute-start.9 = (bf16[2,64,1024]{2,1,0:T(8,128)(2,1)S(1)}, bf16[2,64,1024]{2,1,0:T(8,128)(2,1)}, u32[]{:S(2)}, u32[]{:S(2)}) collective-permute-start(bf16[2,64,1024]{2,1,0:T(8,128)(2,1)S(1)} %pad_maximum_fusion.4), channel_id=1, source_target_pairs={{0,112},{16,0},{32,16},{48,32},{64,48},{80,64},{96,80},{112,96},{1... | collective-permute-start | bytes 786440 | tf_op jit(solution)/shard_map/input_grad/ppermute | solution.py:27
  80.7 6.5 %copy-start.9 = (bf16[2,64,1024]{2,1,0:T(8,128)(2,1)}, bf16[2,64,1024]{2,1,0:T(8,128)(2,1)S(1)}, u32[]{:S(2)}) copy-start(bf16[2,64,1024]{2,1,0:T(8,128)(2,1)S(1)} %collective-permute-done.7) | copy-start | bytes 786436
  87.2 0.7 copy-start.10
  93.7 1.0 copy-start.2
  93.7 1.2 copy-start.4
  96.7 1.4 copy-start
  101.8 40.7 %all-to-all-start.1 = ((bf16[8,128,1024]{2,1,0:T(8,128)(2,1)}), bf16[8,128,1024]{2,1,0:T(8,128)(2,1)}, u32[]{:S(2)}, u32[]{:S(2)}) async-start(bf16[8,128,1024]{2,1,0:T(8,128)(2,1)} %bitcast.74), calls=%async_computation.1 | async-start | bytes 4194304 | tf_op jit(solution)/shard_map/input_grad/all_to_all | solution.py:137
  112.2 11.1 %collective-permute-start.12 = (bf16[2,2,32,1024]{3,2,1,0:T(8,128)(2,1)S(1)}, bf16[2,2,32,1024]{3,2,1,0:T(8,128)(2,1)S(1)}, u32[]{:S(2)}, u32[]{:S(2)}) collective-permute-start(bf16[2,2,32,1024]{3,2,1,0:T(8,128)(2,1)S(1)} %get-tuple-element.31), channel_id=1, source_target_pairs={{0,112},{16,0},{32,16},{48,32},{64,48},{80,64},{96,80},{112,96},{1... | collective-permute-start | bytes 786440 | tf_op jit(solution)/shard_map/weight_grad/ppermute | solution.py:27
  114.2 11.6 %collective-permute-start.11 = (bf16[2,2,32,1024]{3,2,1,0:T(8,128)(2,1)S(1)}, bf16[2,2,32,1024]{3,2,1,0:T(8,128)(2,1)S(1)}, u32[]{:S(2)}, u32[]{:S(2)}) collective-permute-start(bf16[2,2,32,1024]{3,2,1,0:T(8,128)(2,1)S(1)} %get-tuple-element.32), channel_id=1, source_target_pairs={{0,16},{16,32},{32,48},{48,64},{64,80},{80,96},{96,112},{112,0},{1... | collective-permute-start | bytes 786440 | tf_op jit(solution)/shard_map/weight_grad/ppermute | solution.py:27
  118.1 13.4 %collective-permute-start.10 = (bf16[2,2,32,1024]{3,2,1,0:T(8,128)(2,1)S(1)}, bf16[2,2,32,1024]{3,2,1,0:T(8,128)(2,1)S(1)}, u32[]{:S(2)}, u32[]{:S(2)}) collective-permute-start(bf16[2,2,32,1024]{3,2,1,0:T(8,128)(2,1)S(1)} %get-tuple-element.30), channel_id=1, source_target_pairs={{0,32},{16,112},{32,64},{48,16},{64,96},{80,48},{96,0},{112,80},{1... | collective-permute-start | bytes 786440 | tf_op jit(solution)/shard_map/weight_grad/ppermute | solution.py:27
  131.7 10.8 %collective-permute-start.13 = (bf16[2,32,1024]{2,1,0:T(8,128)(2,1)S(1)}, bf16[2,32,1024]{2,1,0:T(8,128)(2,1)S(1)}, u32[]{:S(2)}, u32[]{:S(2)}) collective-permute-start(bf16[2,32,1024]{2,1,0:T(8,128)(2,1)S(1)} %fusion.12), channel_id=1, source_target_pairs={{0,64},{64,0},{1,65},{65,1},{2,66},{66,2},{3,67},{67,3},{4,68},{68... | collective-permute-start | bytes 393224 | tf_op jit(solution)/shard_map/weight_grad/ppermute | solution.py:20
  174.4 35.8 %all-to-all-start.3 = ((bf16[16,32,1024]{2,1,0:T(8,128)(2,1)}), bf16[16,32,1024]{2,1,0:T(8,128)(2,1)S(1)}, u32[]{:S(2)}, u32[]{:S(2)}) async-start(bf16[16,32,1024]{2,1,0:T(8,128)(2,1)} %broadcast_in_dim.5), calls=%async_computation.3 | async-start | bytes 2097152 | tf_op jit(solution)/shard_map/weight_grad/all_to_all | solution.py:163

commit v3 on v2

--- a/solution.py
+++ b/solution.py
@@ -95,7 +95,6 @@
 
     with jax.named_scope("key_grads"):
         both = pair_in_order(key_grad[None], key_other[None], zp, 0)
-        both, theirs = lax.optimization_barrier((both, theirs))
         shares = pair_in_order(theirs[None], swapped(theirs, "yh")[None], yh, 0)
         from_left = lax.ppermute(both, "x", [(i, (i + 1) % nx) for i in range(nx)])
         from_right = lax.ppermute(both, "x", [(i, (i - 1) % nx) for i in range(nx)])

time: 213 us -> 208 us (0.977)
  the two profiles are of different devices: /device:TPU:8 before, /device:TPU:10 now
where the time goes in v3:
time: 208 us; the launch traced here: 206 us
  starting transfers between devices  86.5 us (42%)
  waiting for transfers between devices  46.3 us (22%)
  blocking collectives  27 us (13%)
  local copies, waits for them, and re-layouts  18.2 us (9%)
  other arithmetic  15.7 us (8%)
  matrix products  7.62 us (4%)
  Pallas kernels  3.78 us (2%)
    ppermute x5, starting transfers between devices, swapped(): return lax.ppermute(value, axis, [(0, 1), (1, 0)])  32.8 us
    all_to_all x1, blocking collectives, local(): lax.all_to_all(spread.reshape(2 * nt, piece, cols), ('zt', 'zh'), 0, 0, t...  27 us
    ppermute x6, starting transfers between devices, around_y(): return lax.ppermute(value, ('yh', 'yl'), [(i, target(i)) for i in range(8)])  21.7 us
    ppermute x6, waiting for transfers between devices, around_y(): return lax.ppermute(value, ('yh', 'yl'), [(i, target(i)) for i in range(8)])  18.6 us
    ppermute x5, waiting for transfers between devices, swapped(): return lax.ppermute(value, axis, [(0, 1), (1, 0)])  15.4 us
    all_to_all x1, waiting for transfers between devices, local(): gathered = lax.all_to_all(spread, ('zp', 'yh', 'yl'), 0, 0, tiled=True)  12.4 us
    reshape x3, local copies, waits for them, and re-layouts, local(): back.reshape(2, nx, tokens, 2, rows).transpose(2, 1, 3, 0, 4)  12.3 us
    all_to_all x1, starting transfers between devices, local(): gathered = lax.all_to_all(spread, ('zp', 'yh', 'yl'), 0, 0, tiled=True)  11.3 us
  transfers between devices with their start and end apart: 17, of which 9 were waited for; matrix products, arithmetic and copies ran while one was open for 16% of the time, Pallas kernels for 2%

profile of v3, /device:TPU:10, one launch (start us, length us, event | category | flops | bytes accessed | tf_op | source)
XLA Modules:
  0.0 206.3 jit_solution(6053536220787804206)
XLA Ops:
  0.6 4.3 %collective-permute-start = (bf16[128,1024]{1,0:T(8,128)(2,1)}, bf16[128,1024]{1,0:T(8,128)(2,1)S(1)}, u32[]{:S(2)}, u32[]{:S(2)}) collective-permute-start(bf16[128,1024]{1,0:T(8,128)(2,1)} %param.5), channel_id=1, source_target_pairs={{0,128},{128,0},{1,129},{129,1},{2,130},{130,2},{3,131},{131,3},{4... | collective-permute-start | bytes 786440 | tf_op jit(solution)/shard_map/inputs/ppermute | solution.py:20
  4.9 6.5 %collective-permute-done = bf16[128,1024]{1,0:T(8,128)(2,1)S(1)} collective-permute-done((bf16[128,1024]{1,0:T(8,128)(2,1)}, bf16[128,1024]{1,0:T(8,128)(2,1)S(1)}, u32[]{:S(2)}, u32[]{:S(2)}) %collective-permute-start) | collective-permute-done | bytes 262176 | tf_op jit(solution)/shard_map/inputs/ppermute | solution.py:20
  11.4 1.0 select_bitcast_fusion.11
  12.4 0.9 pad_maximum_fusion.3
  13.3 2.4 %collective-permute-start.2 = (bf16[2,128,1024]{2,1,0:T(8,128)(2,1)}, bf16[2,128,1024]{2,1,0:T(8,128)(2,1)S(1)}, u32[]{:S(2)}, u32[]{:S(2)}) collective-permute-start(bf16[2,128,1024]{2,1,0:T(8,128)(2,1)} %pad_maximum_fusion.3), channel_id=1, source_target_pairs={{0,12},{4,0},{8,4},{12,8},{1,13},{5,1},{9,5},{13,9},{2,14},{6,2},{... | collective-permute-start | bytes 1572872 | tf_op jit(solution)/shard_map/key_grads/ppermute | solution.py:100
  15.8 1.5 fusion.5
  17.3 14.8 %collective-permute-start.4 = (bf16[64,1024]{1,0:T(8,128)(2,1)S(1)}, bf16[64,1024]{1,0:T(8,128)(2,1)S(1)}, u32[]{:S(2)}, u32[]{:S(2)}) collective-permute-start(bf16[64,1024]{1,0:T(8,128)(2,1)S(1)} %constant_dynamic-slice_fusion), channel_id=1, source_target_pairs={{0,2},{2,0},{1,3},{3,1},{4,6},{6,4},{5,7},{7,5},{8,10},{10,8},{9,1... | collective-permute-start | bytes 393224 | tf_op jit(solution)/shard_map/inputs/ppermute | solution.py:20
  32.1 3.4 %collective-permute-start.1 = (bf16[2,128,1024]{2,1,0:T(8,128)(2,1)}, bf16[2,128,1024]{2,1,0:T(8,128)(2,1)S(1)}, u32[]{:S(2)}, u32[]{:S(2)}) collective-permute-start(bf16[2,128,1024]{2,1,0:T(8,128)(2,1)} %pad_maximum_fusion.3), channel_id=1, source_target_pairs={{0,4},{4,8},{8,12},{12,0},{1,5},{5,9},{9,13},{13,1},{2,6},{6,10},{... | collective-permute-start | bytes 1572872 | tf_op jit(solution)/shard_map/key_grads/ppermute | solution.py:99
  35.6 3.2 %collective-permute-start.3 = (bf16[2,128,1024]{2,1,0:T(8,128)(2,1)S(1)}, bf16[2,128,1024]{2,1,0:T(8,128)(2,1)S(1)}, u32[]{:S(2)}, u32[]{:S(2)}) collective-permute-start(bf16[2,128,1024]{2,1,0:T(8,128)(2,1)S(1)} %collective-permute-done.2), channel_id=1, source_target_pairs={{0,12},{4,0},{8,4},{12,8},{1,13},{5,1},{9,5},{13,9},{2,14},{6,2},{... | collective-permute-start | bytes 1572872 | tf_op jit(solution)/shard_map/key_grads/ppermute | solution.py:101
  38.8 6.8 %collective-permute-start.5 = (bf16[64,1024]{1,0:T(8,128)(2,1)S(1)}, bf16[64,1024]{1,0:T(8,128)(2,1)}, u32[]{:S(2)}, u32[]{:S(2)}) collective-permute-start(bf16[64,1024]{1,0:T(8,128)(2,1)S(1)} %collective-permute-done.4), channel_id=1, source_target_pairs={{0,64},{64,0},{1,65},{65,1},{2,66},{66,2},{3,67},{67,3},{4,68},{68... | collective-permute-start | bytes 393224 | tf_op jit(solution)/shard_map/key_grads/ppermute | solution.py:20
  45.6 3.8 %key_grads.1 = bf16[16,128,512]{2,1,0:T(8,128)(2,1)} custom-call(bf16[128,8192]{1,0:T(8,128)(2,1)} %source.1), custom_call_target="tpu_custom_call" | custom-call | bytes 4194304 | tf_op jit(solution)/shard_map/key_grads/pallas_call | solution.py:48
  49.4 1.5 collective-permute-done.5
  50.9 0.9 select_bitcast_fusion.13
  52.5 0.8 copy-done.8
  53.3 6.9 %all-to-all-start = ((bf16[16,128,512]{2,1,0:T(8,128)(2,1)}), bf16[16,128,512]{2,1,0:T(8,128)(2,1)}, u32[]{:S(2)}, u32[]{:S(2)}) async-start(bf16[16,128,512]{2,1,0:T(8,128)(2,1)} %key_grads.1), calls=%async_computation | async-start | bytes 4194304 | tf_op jit(solution)/shard_map/inputs/all_to_all | solution.py:116
  60.4 0.9 copy-done.9
  61.3 1.6 select_bitcast_fusion.5
  63.0 1.6 pad_maximum_fusion.1
  64.5 2.1 %collective-permute-start.6 = (bf16[2,4,128,1024]{3,2,1,0:T(8,128)(2,1)}, bf16[2,4,128,1024]{3,2,1,0:T(8,128)(2,1)}, u32[]{:S(2)}, u32[]{:S(2)}) collective-permute-start(bf16[2,4,128,1024]{3,2,1,0:T(8,128)(2,1)} %pad_maximum_fusion.1), channel_id=1, source_target_pairs={{0,1},{1,0},{2,3},{3,2},{4,5},{5,4},{6,7},{7,6},{8,9},{9,8},{10,11... | collective-permute-start | bytes 6291464 | tf_op jit(solution)/shard_map/key_grads/ppermute | solution.py:20
  66.6 4.1 %collective-permute-start.7 = (bf16[2,64,1024]{2,1,0:T(8,128)(2,1)S(1)}, bf16[2,64,1024]{2,1,0:T(8,128)(2,1)S(1)}, u32[]{:S(2)}, u32[]{:S(2)}) collective-permute-start(bf16[2,64,1024]{2,1,0:T(8,128)(2,1)S(1)} %copy-done.10), channel_id=1, source_target_pairs={{0,16},{16,32},{32,48},{48,64},{64,80},{80,96},{96,112},{112,0},{1... | collective-permute-start | bytes 786440 | tf_op jit(solution)/shard_map/input_grad/ppermute | solution.py:27
  70.8 3.7 %collective-permute-start.8 = (bf16[2,64,1024]{2,1,0:T(8,128)(2,1)S(1)}, bf16[2,64,1024]{2,1,0:T(8,128)(2,1)S(1)}, u32[]{:S(2)}, u32[]{:S(2)}) collective-permute-start(bf16[2,64,1024]{2,1,0:T(8,128)(2,1)S(1)} %copy-done.10), channel_id=1, source_target_pairs={{0,32},{16,112},{32,64},{48,16},{64,96},{80,48},{96,0},{112,80},{1... | collective-permute-start | bytes 786440 | tf_op jit(solution)/shard_map/input_grad/ppermute | solution.py:27
  74.5 2.8 %collective-permute-start.9 = (bf16[2,64,1024]{2,1,0:T(8,128)(2,1)S(1)}, bf16[2,64,1024]{2,1,0:T(8,128)(2,1)}, u32[]{:S(2)}, u32[]{:S(2)}) collective-permute-start(bf16[2,64,1024]{2,1,0:T(8,128)(2,1)S(1)} %copy-done.10), channel_id=1, source_target_pairs={{0,112},{16,0},{32,16},{48,32},{64,48},{80,64},{96,80},{112,96},{1... | collective-permute-start | bytes 786440 | tf_op jit(solution)/shard_map/input_grad/ppermute | solution.py:27
  77.4 5.0 %collective-permute-done.7 = bf16[2,64,1024]{2,1,0:T(8,128)(2,1)S(1)} collective-permute-done((bf16[2,64,1024]{2,1,0:T(8,128)(2,1)S(1)}, bf16[2,64,1024]{2,1,0:T(8,128)(2,1)S(1)}, u32[]{:S(2)}, u32[]{:S(2)}) %collective-permute-start.7) | collective-permute-done | bytes 262176 | tf_op jit(solution)/shard_map/input_grad/ppermute | solution.py:27
  82.4 1.3 collective-permute-done.8
  84.4 4.4 %collective-permute-done.9 = bf16[2,64,1024]{2,1,0:T(8,128)(2,1)} collective-permute-done((bf16[2,64,1024]{2,1,0:T(8,128)(2,1)S(1)}, bf16[2,64,1024]{2,1,0:T(8,128)(2,1)}, u32[]{:S(2)}, u32[]{:S(2)}) %collective-permute-start.9) | collective-permute-done | bytes 262176 | tf_op jit(solution)/shard_map/input_grad/ppermute | solution.py:27
  88.8 1.2 select_bitcast_fusion.9
  90.5 0.8 copy-done.2
  91.5 1.8 select_bitcast_fusion
  93.5 1.2 copy-done
  94.7 3.7 %fusion.6 = bf16[1024,1024]{1,0:T(8,128)(2,1)} fusion(bf16[1024,1024]{1,0:T(8,128)(2,1)S(1)} %bitcast.73, bf16[512,1024]{1,0:T(8,128)(2,1)S(1)} %get-tuple-element.21, bf16[512,1024]{1,0:T(8,128)(2,1)S(1)} %get-tuple-element.20), kind=kOutput, calls=%fused_computation.15 | convolution fusion | flops 2152726528 | bytes 6291456 | tf_op jit(solution)/shard_map/input_grad/dot_general | solution.py:129
  98.4 4.8 %all-to-all-start.1 = ((bf16[8,128,1024]{2,1,0:T(8,128)(2,1)}), bf16[8,128,1024]{2,1,0:T(8,128)(2,1)}, u32[]{:S(2)}, u32[]{:S(2)}) async-start(bf16[8,128,1024]{2,1,0:T(8,128)(2,1)} %bitcast.74), calls=%async_computation.1 | async-start | bytes 4194304 | tf_op jit(solution)/shard_map/input_grad/all_to_all | solution.py:136
  103.2 2.0 pad_maximum_fusion
  105.1 3.9 %multiply_convert_fusion = bf16[512,1024]{1,0:T(8,128)(2,1)S(1)} fusion(bf16[2048,512]{1,0:T(8,128)(2,1)} %bitcast.20, bf16[2048,1024]{1,0:T(8,128)(2,1)S(1)} %bitcast.72), kind=kOutput, calls=%fused_computation.12 | convolution fusion | flops 2148532224 | bytes 7340032 | tf_op jit(solution)/shard_map/weight_grad/dot_general | solution.py:141
  109.2 1.9 collective-permute-start.12
  111.1 3.9 %collective-permute-start.11 = (bf16[2,2,32,1024]{3,2,1,0:T(8,128)(2,1)S(1)}, bf16[2,2,32,1024]{3,2,1,0:T(8,128)(2,1)S(1)}, u32[]{:S(2)}, u32[]{:S(2)}) collective-permute-start(bf16[2,2,32,1024]{3,2,1,0:T(8,128)(2,1)S(1)} %get-tuple-element.27), channel_id=1, source_target_pairs={{0,16},{16,32},{32,48},{48,64},{64,80},{80,96},{96,112},{112,0},{1... | collective-permute-start | bytes 786440 | tf_op jit(solution)/shard_map/weight_grad/ppermute | solution.py:27
  115.0 5.2 %collective-permute-start.10 = (bf16[2,2,32,1024]{3,2,1,0:T(8,128)(2,1)S(1)}, bf16[2,2,32,1024]{3,2,1,0:T(8,128)(2,1)S(1)}, u32[]{:S(2)}, u32[]{:S(2)}) collective-permute-start(bf16[2,2,32,1024]{3,2,1,0:T(8,128)(2,1)S(1)} %get-tuple-element.25), channel_id=1, source_target_pairs={{0,32},{16,112},{32,64},{48,16},{64,96},{80,48},{96,0},{112,80},{1... | collective-permute-start | bytes 786440 | tf_op jit(solution)/shard_map/weight_grad/ppermute | solution.py:27
  120.2 2.4 %collective-permute-done.11 = bf16[2,2,32,1024]{3,2,1,0:T(8,128)(2,1)S(1)} collective-permute-done((bf16[2,2,32,1024]{3,2,1,0:T(8,128)(2,1)S(1)}, bf16[2,2,32,1024]{3,2,1,0:T(8,128)(2,1)S(1)}, u32[]{:S(2)}, u32[]{:S(2)}) %collective-permute-start.11) | collective-permute-done | bytes 262176 | tf_op jit(solution)/shard_map/weight_grad/ppermute | solution.py:27
  122.6 5.5 %collective-permute-done.10 = bf16[2,2,32,1024]{3,2,1,0:T(8,128)(2,1)S(1)} collective-permute-done((bf16[2,2,32,1024]{3,2,1,0:T(8,128)(2,1)S(1)}, bf16[2,2,32,1024]{3,2,1,0:T(8,128)(2,1)S(1)}, u32[]{:S(2)}, u32[]{:S(2)}) %collective-permute-start.10) | collective-permute-done | bytes 262176 | tf_op jit(solution)/shard_map/weight_grad/ppermute | solution.py:27
  128.2 4.7 %collective-permute-start.13 = (bf16[2,32,1024]{2,1,0:T(8,128)(2,1)S(1)}, bf16[2,32,1024]{2,1,0:T(8,128)(2,1)S(1)}, u32[]{:S(2)}, u32[]{:S(2)}) collective-permute-start(bf16[2,32,1024]{2,1,0:T(8,128)(2,1)S(1)} %fusion.12), channel_id=1, source_target_pairs={{0,64},{64,0},{1,65},{65,1},{2,66},{66,2},{3,67},{67,3},{4,68},{68... | collective-permute-start | bytes 393224 | tf_op jit(solution)/shard_map/weight_grad/ppermute | solution.py:20
  133.0 7.4 %collective-permute-done.13 = bf16[2,32,1024]{2,1,0:T(8,128)(2,1)S(1)} collective-permute-done((bf16[2,32,1024]{2,1,0:T(8,128)(2,1)S(1)}, bf16[2,32,1024]{2,1,0:T(8,128)(2,1)S(1)}, u32[]{:S(2)}, u32[]{:S(2)}) %collective-permute-start.13) | collective-permute-done | bytes 131104 | tf_op jit(solution)/shard_map/weight_grad/ppermute | solution.py:20
  140.5 27.0 %all_to_all.20 = bf16[6,32,1024]{2,1,0:T(8,128)(2,1)S(1)} all-to-all(bf16[6,32,1024]{2,1,0:T(8,128)(2,1)S(1)} %bitcast.75), channel_id=1, replica_groups=mesh['zt'=3,'zp'=2,'yh'=2,'yl'=4,'x'=4,'zh'=2,'c'=2] {'zt','zh'}, dimensions={0} | all-to-all | bytes 786432 | tf_op jit(solution)/shard_map/weight_grad/all_to_all | solution.py:157
  167.6 1.1 broadcast_in_dim.5
  168.7 11.3 %all-to-all-start.3 = ((bf16[16,32,1024]{2,1,0:T(8,128)(2,1)}), bf16[16,32,1024]{2,1,0:T(8,128)(2,1)S(1)}, u32[]{:S(2)}, u32[]{:S(2)}) async-start(bf16[16,32,1024]{2,1,0:T(8,128)(2,1)} %broadcast_in_dim.5), calls=%async_computation.3 | async-start | bytes 2097152 | tf_op jit(solution)/shard_map/weight_grad/all_to_all | solution.py:162
  180.0 3.3 %reshape.56 = bf16[2,4,128,2,512]{4,3,2,1,0:T(2,128)(2,1)S(1)} reshape(bf16[8,128,1024]{2,1,0:T(8,128)(2,1)} %all-to-all-done.1) | data formatting | bytes 4194304 | tf_op jit(solution)/shard_map/input_grad/reshape | solution.py:167
  183.3 4.6 %copy.19 = bf16[2,4,128,2,512]{4,0,3,1,2:T(2,128)(2,1)} copy(bf16[2,4,128,2,512]{4,3,2,1,0:T(2,128)(2,1)S(1)} %reshape.56) | data formatting | bytes 4194304 | tf_op jit(solution)/shard_map/input_grad/reshape | solution.py:167
  187.9 4.5 %reshape.57 = bf16[128,8192]{1,0:T(8,128)(2,1)} reshape(bf16[128,4,2,2,512]{4,3,2,1,0:T(2,128)(2,1)} %bitcast.71) | data formatting | bytes 4194304 | tf_op jit(solution)/shard_map/input_grad/reshape | solution.py:167
  192.3 12.4 %all-to-all-done.3 = bf16[16,32,1024]{2,1,0:T(8,128)(2,1)S(1)} async-done(((bf16[16,32,1024]{2,1,0:T(8,128)(2,1)}), bf16[16,32,1024]{2,1,0:T(8,128)(2,1)S(1)}, u32[]{:S(2)}, u32[]{:S(2)}) %all-to-all-start.3) | async-done | bytes 1048608 | tf_op jit(solution)/shard_map/weight_grad/all_to_all | solution.py:162
  204.7 1.6 bitcast_convert_fusion
  (45 shorter events, 2.7 us)
Async XLA Ops:
  0.6 15.1 %copy-start.13 = (f32[4,1024]{1,0:T(4,128)S(1)}, f32[4,1024]{1,0:T(4,128)}, u32[]{:S(2)}) copy-start(f32[4,1024]{1,0:T(4,128)} %param.7) | copy-start | bytes 49156
  0.6 10.8 %collective-permute-start = (bf16[128,1024]{1,0:T(8,128)(2,1)}, bf16[128,1024]{1,0:T(8,128)(2,1)S(1)}, u32[]{:S(2)}, u32[]{:S(2)}) collective-permute-start(bf16[128,1024]{1,0:T(8,128)(2,1)} %param.5), channel_id=1, source_target_pairs={{0,128},{128,0},{1,129},{129,1},{2,130},{130,2},{3,131},{131,3},{4... | collective-permute-start | bytes 786440 | tf_op jit(solution)/shard_map/inputs/ppermute | solution.py:20
  12.4 47.8 %copy-start.5 = (bf16[1,128,1024]{2,1,0:T(8,128)(2,1)}, bf16[1,128,1024]{2,1,0:T(8,128)(2,1)S(1)}, u32[]{:S(2)}) copy-start(bf16[1,128,1024]{2,1,0:T(8,128)(2,1)S(1)} %get-tuple-element.33) | copy-start | bytes 786436
  13.3 22.2 %collective-permute-start.2 = (bf16[2,128,1024]{2,1,0:T(8,128)(2,1)}, bf16[2,128,1024]{2,1,0:T(8,128)(2,1)S(1)}, u32[]{:S(2)}, u32[]{:S(2)}) collective-permute-start(bf16[2,128,1024]{2,1,0:T(8,128)(2,1)} %pad_maximum_fusion.3), channel_id=1, source_target_pairs={{0,12},{4,0},{8,4},{12,8},{1,13},{5,1},{9,5},{13,9},{2,14},{6,2},{... | collective-permute-start | bytes 1572872 | tf_op jit(solution)/shard_map/key_grads/ppermute | solution.py:100
  17.3 21.5 %collective-permute-start.4 = (bf16[64,1024]{1,0:T(8,128)(2,1)S(1)}, bf16[64,1024]{1,0:T(8,128)(2,1)S(1)}, u32[]{:S(2)}, u32[]{:S(2)}) collective-permute-start(bf16[64,1024]{1,0:T(8,128)(2,1)S(1)} %constant_dynamic-slice_fusion), channel_id=1, source_target_pairs={{0,2},{2,0},{1,3},{3,1},{4,6},{6,4},{5,7},{7,5},{8,10},{10,8},{9,1... | collective-permute-start | bytes 393224 | tf_op jit(solution)/shard_map/inputs/ppermute | solution.py:20
  32.1 20.4 %collective-permute-start.1 = (bf16[2,128,1024]{2,1,0:T(8,128)(2,1)}, bf16[2,128,1024]{2,1,0:T(8,128)(2,1)S(1)}, u32[]{:S(2)}, u32[]{:S(2)}) collective-permute-start(bf16[2,128,1024]{2,1,0:T(8,128)(2,1)} %pad_maximum_fusion.3), channel_id=1, source_target_pairs={{0,4},{4,8},{8,12},{12,0},{1,5},{5,9},{9,13},{13,1},{2,6},{6,10},{... | collective-permute-start | bytes 1572872 | tf_op jit(solution)/shard_map/key_grads/ppermute | solution.py:99
  35.5 24.7 %copy-start.6 = (bf16[2,128,1024]{2,1,0:T(8,128)(2,1)}, bf16[2,128,1024]{2,1,0:T(8,128)(2,1)S(1)}, u32[]{:S(2)}) copy-start(bf16[2,128,1024]{2,1,0:T(8,128)(2,1)S(1)} %collective-permute-done.2) | copy-start | bytes 1572868
  35.6 17.0 %collective-permute-start.3 = (bf16[2,128,1024]{2,1,0:T(8,128)(2,1)S(1)}, bf16[2,128,1024]{2,1,0:T(8,128)(2,1)S(1)}, u32[]{:S(2)}, u32[]{:S(2)}) collective-permute-start(bf16[2,128,1024]{2,1,0:T(8,128)(2,1)S(1)} %collective-permute-done.2), channel_id=1, source_target_pairs={{0,12},{4,0},{8,4},{12,8},{1,13},{5,1},{9,5},{13,9},{2,14},{6,2},{... | collective-permute-start | bytes 1572872 | tf_op jit(solution)/shard_map/key_grads/ppermute | solution.py:101
  38.8 12.1 %collective-permute-start.5 = (bf16[64,1024]{1,0:T(8,128)(2,1)S(1)}, bf16[64,1024]{1,0:T(8,128)(2,1)}, u32[]{:S(2)}, u32[]{:S(2)}) collective-permute-start(bf16[64,1024]{1,0:T(8,128)(2,1)S(1)} %collective-permute-done.4), channel_id=1, source_target_pairs={{0,64},{64,0},{1,65},{65,1},{2,66},{66,2},{3,67},{67,3},{4,68},{68... | collective-permute-start | bytes 393224 | tf_op jit(solution)/shard_map/key_grads/ppermute | solution.py:20
  52.5 7.7 %copy-start.7 = (bf16[2,128,1024]{2,1,0:T(8,128)(2,1)}, bf16[2,128,1024]{2,1,0:T(8,128)(2,1)S(1)}, u32[]{:S(2)}) copy-start(bf16[2,128,1024]{2,1,0:T(8,128)(2,1)S(1)} %collective-permute-done.1) | copy-start | bytes 1572868
  52.5 0.8 copy-start.8
  53.3 45.0 %all-to-all-start = ((bf16[16,128,512]{2,1,0:T(8,128)(2,1)}), bf16[16,128,512]{2,1,0:T(8,128)(2,1)}, u32[]{:S(2)}, u32[]{:S(2)}) async-start(bf16[16,128,512]{2,1,0:T(8,128)(2,1)} %key_grads.1), calls=%async_computation | async-start | bytes 4194304 | tf_op jit(solution)/shard_map/inputs/all_to_all | solution.py:116
  60.2 1.0 copy-start.9
  61.3 3.3 %copy-start.3 = (bf16[2,1,128,1024]{3,2,1,0:T(8,128)(2,1)}, bf16[2,1,128,1024]{3,2,1,0:T(8,128)(2,1)S(1)}, u32[]{:S(2)}) copy-start(bf16[2,1,128,1024]{3,2,1,0:T(8,128)(2,1)S(1)} %select_bitcast_fusion.4) | copy-start | bytes 1572868
  62.9 1.6 copy-start.1
  62.9 3.7 %copy-start.10 = (bf16[2,64,1024]{2,1,0:T(8,128)(2,1)S(1)}, bf16[2,64,1024]{2,1,0:T(8,128)(2,1)}, u32[]{:S(2)}) copy-start(bf16[2,64,1024]{2,1,0:T(8,128)(2,1)} %pad_maximum_fusion.4) | copy-start | bytes 786436
  64.5 26.0 %collective-permute-start.6 = (bf16[2,4,128,1024]{3,2,1,0:T(8,128)(2,1)}, bf16[2,4,128,1024]{3,2,1,0:T(8,128)(2,1)}, u32[]{:S(2)}, u32[]{:S(2)}) collective-permute-start(bf16[2,4,128,1024]{3,2,1,0:T(8,128)(2,1)} %pad_maximum_fusion.1), channel_id=1, source_target_pairs={{0,1},{1,0},{2,3},{3,2},{4,5},{5,4},{6,7},{7,6},{8,9},{9,8},{10,11... | collective-permute-start | bytes 6291464 | tf_op jit(solution)/shard_map/key_grads/ppermute | solution.py:20
  66.6 15.8 %collective-permute-start.7 = (bf16[2,64,1024]{2,1,0:T(8,128)(2,1)S(1)}, bf16[2,64,1024]{2,1,0:T(8,128)(2,1)S(1)}, u32[]{:S(2)}, u32[]{:S(2)}) collective-permute-start(bf16[2,64,1024]{2,1,0:T(8,128)(2,1)S(1)} %copy-done.10), channel_id=1, source_target_pairs={{0,16},{16,32},{32,48},{48,64},{64,80},{80,96},{96,112},{112,0},{1... | collective-permute-start | bytes 786440 | tf_op jit(solution)/shard_map/input_grad/ppermute | solution.py:27
  70.8 13.0 %collective-permute-start.8 = (bf16[2,64,1024]{2,1,0:T(8,128)(2,1)S(1)}, bf16[2,64,1024]{2,1,0:T(8,128)(2,1)S(1)}, u32[]{:S(2)}, u32[]{:S(2)}) collective-permute-start(bf16[2,64,1024]{2,1,0:T(8,128)(2,1)S(1)} %copy-done.10), channel_id=1, source_target_pairs={{0,32},{16,112},{32,64},{48,16},{64,96},{80,48},{96,0},{112,80},{1... | collective-permute-start | bytes 786440 | tf_op jit(solution)/shard_map/input_grad/ppermute | solution.py:27
  74.5 14.3 %collective-permute-start.9 = (bf16[2,64,1024]{2,1,0:T(8,128)(2,1)S(1)}, bf16[2,64,1024]{2,1,0:T(8,128)(2,1)}, u32[]{:S(2)}, u32[]{:S(2)}) collective-permute-start(bf16[2,64,1024]{2,1,0:T(8,128)(2,1)S(1)} %copy-done.10), channel_id=1, source_target_pairs={{0,112},{16,0},{32,16},{48,32},{64,48},{80,64},{96,80},{112,96},{1... | collective-permute-start | bytes 786440 | tf_op jit(solution)/shard_map/input_grad/ppermute | solution.py:27
  82.4 1.3 copy-start.11
  83.7 0.7 copy-start.12
  90.3 1.0 copy-start.2
  90.3 1.2 copy-start.4
  93.3 1.4 copy-start
  98.4 42.1 %all-to-all-start.1 = ((bf16[8,128,1024]{2,1,0:T(8,128)(2,1)}), bf16[8,128,1024]{2,1,0:T(8,128)(2,1)}, u32[]{:S(2)}, u32[]{:S(2)}) async-start(bf16[8,128,1024]{2,1,0:T(8,128)(2,1)} %bitcast.74), calls=%async_computation.1 | async-start | bytes 4194304 | tf_op jit(solution)/shard_map/input_grad/all_to_all | solution.py:136
  109.2 11.0 %collective-permute-start.12 = (bf16[2,2,32,1024]{3,2,1,0:T(8,128)(2,1)S(1)}, bf16[2,2,32,1024]{3,2,1,0:T(8,128)(2,1)S(1)}, u32[]{:S(2)}, u32[]{:S(2)}) collective-permute-start(bf16[2,2,32,1024]{3,2,1,0:T(8,128)(2,1)S(1)} %get-tuple-element.26), channel_id=1, source_target_pairs={{0,112},{16,0},{32,16},{48,32},{64,48},{80,64},{96,80},{112,96},{1... | collective-permute-start | bytes 786440 | tf_op jit(solution)/shard_map/weight_grad/ppermute | solution.py:27
  111.1 11.5 %collective-permute-start.11 = (bf16[2,2,32,1024]{3,2,1,0:T(8,128)(2,1)S(1)}, bf16[2,2,32,1024]{3,2,1,0:T(8,128)(2,1)S(1)}, u32[]{:S(2)}, u32[]{:S(2)}) collective-permute-start(bf16[2,2,32,1024]{3,2,1,0:T(8,128)(2,1)S(1)} %get-tuple-element.27), channel_id=1, source_target_pairs={{0,16},{16,32},{32,48},{48,64},{64,80},{80,96},{96,112},{112,0},{1... | collective-permute-start | bytes 786440 | tf_op jit(solution)/shard_map/weight_grad/ppermute | solution.py:27
  115.0 13.0 %collective-permute-start.10 = (bf16[2,2,32,1024]{3,2,1,0:T(8,128)(2,1)S(1)}, bf16[2,2,32,1024]{3,2,1,0:T(8,128)(2,1)S(1)}, u32[]{:S(2)}, u32[]{:S(2)}) collective-permute-start(bf16[2,2,32,1024]{3,2,1,0:T(8,128)(2,1)S(1)} %get-tuple-element.25), channel_id=1, source_target_pairs={{0,32},{16,112},{32,64},{48,16},{64,96},{80,48},{96,0},{112,80},{1... | collective-permute-start | bytes 786440 | tf_op jit(solution)/shard_map/weight_grad/ppermute | solution.py:27
  128.2 12.2 %collective-permute-start.13 = (bf16[2,32,1024]{2,1,0:T(8,128)(2,1)S(1)}, bf16[2,32,1024]{2,1,0:T(8,128)(2,1)S(1)}, u32[]{:S(2)}, u32[]{:S(2)}) collective-permute-start(bf16[2,32,1024]{2,1,0:T(8,128)(2,1)S(1)} %fusion.12), channel_id=1, source_target_pairs={{0,64},{64,0},{1,65},{65,1},{2,66},{66,2},{3,67},{67,3},{4,68},{68... | collective-permute-start | bytes 393224 | tf_op jit(solution)/shard_map/weight_grad/ppermute | solution.py:20
  168.7 36.0 %all-to-all-start.3 = ((bf16[16,32,1024]{2,1,0:T(8,128)(2,1)}), bf16[16,32,1024]{2,1,0:T(8,128)(2,1)S(1)}, u32[]{:S(2)}, u32[]{:S(2)}) async-start(bf16[16,32,1024]{2,1,0:T(8,128)(2,1)} %broadcast_in_dim.5), calls=%async_computation.3 | async-start | bytes 2097152 | tf_op jit(solution)/shard_map/weight_grad/all_to_all | solution.py:162
